TPU v7x, 512 devices: a whole 4x4x16 slice. The times are simulated.
512 devices in a mesh: member: 16 (over z_hi, y), gx: 8 (over z_lo, core), gy: 4 (over x).
Axes of the slice: x: 4, y: 4, z: 16 (z_hi: 4, z_lo: 4; z = z_hi * 4 + z_lo), core: 2. Of those that a mesh axis runs over, the one named last changes fastest.
Arguments:
- density: float32 [16, 64, 256, 512], P('member', None, 'gx', 'gy'), may hold values from 0.1 to 2
- turn_rate: bfloat16 [16, 64, 256, 512], P('member', None, 'gx', 'gy'), may hold values from -0.19921875 to 0.19921875
- value_init: float32 [64, 256, 512], P(None, 'gx', 'gy'), may hold values from -33 to 3
- labels: int32 [256, 512], P('gx', 'gy'), may hold values from 0 to 7
- counts: int32 [16], replicated, may hold values from 1 to 16
- kernel: float32 [64, 64], replicated, may hold values from -4 to 4
Outputs:
- moved: float32 [16, 64, 256, 512], P('member', None, 'gx', 'gy')
- values: float32 [64, 256, 512], P(None, 'gx', 'gy')
All inputs are finite; a program needn't handle non-finite values.
Results may differ from a plain program's by a relative error of at most 0.0003.
Values may be sent and summed in bfloat16 or wider, within the bound.
A program may use at most 64 MiB of HBM per device.

v0:
```python
import jax
import jax.numpy as jnp
from jax import lax
from jax.sharding import PartitionSpec as P

speed_scale = 0.55
temper = 0.1
time_step = 0.5
turn_cost = 0.5


def extended(block, sides, width):
    for axis, dim in sides:
        count = lax.axis_size(axis)
        forward = [(i, i + 1) for i in range(count - 1)]
        backward = [(target, source) for source, target in forward]
        low = lax.ppermute(
            lax.slice_in_dim(block, block.shape[dim] - width, None, axis=dim), axis, forward
        )
        high = lax.ppermute(lax.slice_in_dim(block, 0, width, axis=dim), axis, backward)
        block = jnp.concatenate([low, block, high], axis=dim)
    return block


def heading_tables(count):
    angles = jnp.arange(count).astype(jnp.float32) * (2.0 * jnp.pi / count)
    along_x = (speed_scale * jnp.cos(angles)).reshape(count, 1, 1)
    along_y = (speed_scale * jnp.sin(angles)).reshape(count, 1, 1)
    spread = angles[:, None] - angles[None, :]
    coupling = jnp.exp(-turn_cost * (1.0 - jnp.cos(spread)) / temper)
    return (
        jnp.maximum(along_x, 0.0),
        jnp.maximum(-along_x, 0.0),
        jnp.maximum(along_y, 0.0),
        jnp.maximum(-along_y, 0.0),
        coupling,
    )


def edge_weights(opened):
    center = opened[1:-1, 1:-1]
    return (
        center * opened[2:, 1:-1],
        center * opened[:-2, 1:-1],
        center * opened[1:-1, 2:],
        center * opened[1:-1, :-2],
    )


def transport(masses, opened, turning, absorb):
    east_rate, west_rate, north_rate, south_rate, coupling = heading_tables(masses.shape[0])
    to_east, to_west, to_north, to_south = edge_weights(opened)
    center = masses[:, 1:-1, 1:-1]
    leaving = center * (
        east_rate * to_east + west_rate * to_west + north_rate * to_north + south_rate * to_south
    )
    arriving = (
        east_rate * to_west * masses[:, :-2, 1:-1]
        + west_rate * to_east * masses[:, 2:, 1:-1]
        + north_rate * to_south * masses[:, 1:-1, :-2]
        + south_rate * to_north * masses[:, 1:-1, 2:]
    )
    turn_up = jnp.maximum(turning, 0.0)
    turn_down = jnp.maximum(-turning, 0.0)
    rotated = (
        jnp.roll(turn_up * center, 1, axis=0)
        + jnp.roll(turn_down * center, -1, axis=0)
        - (turn_up + turn_down) * center
    )
    return (center - leaving + arriving + rotated) * (1.0 - absorb)


def best_reply(widened, opened, running, absorb):
    east_rate, west_rate, north_rate, south_rate, coupling = heading_tables(widened.shape[0])
    to_east, to_west, to_north, to_south = edge_weights(opened)
    center = widened[:, 1:-1, 1:-1]
    moves = (
        center
        + east_rate * to_east * (widened[:, 2:, 1:-1] - center)
        + west_rate * to_west * (widened[:, :-2, 1:-1] - center)
        + north_rate * to_north * (widened[:, 1:-1, 2:] - center)
        + south_rate * to_south * (widened[:, 1:-1, :-2] - center)
    )
    lowest = jnp.min(moves, axis=0)
    scaled = jnp.exp((lowest - moves) / temper)
    count = moves.shape[0]
    summed = jnp.dot(coupling, scaled.reshape(count, -1), precision=lax.Precision.HIGHEST).reshape(
        moves.shape
    )
    return (time_step * running + lowest - temper * jnp.log(summed)) * (1.0 - absorb)


def congestion(kernel, mixed):
    count = mixed.shape[0]
    return 1.0 + jnp.dot(kernel, mixed.reshape(count, -1), precision=lax.Precision.HIGHEST).reshape(
        mixed.shape
    )


def shards(density, turn_rate, value_init, labels, counts, kernel):
    marks = jnp.stack([(labels != 1).astype(jnp.float32), (labels == 2).astype(jnp.float32)])
    margin = 1
    rimmed = extended(marks, (("gx", 1), ("gy", 2)), margin)
    opened = rimmed[0]
    absorb = marks[1]
    masses = density[0]
    turning = turn_rate[0].astype(jnp.float32)
    for repeat in range(2):
        widened = extended(masses, (("gx", 1), ("gy", 2)), 1)
        masses = transport(widened, opened, turning, absorb)
    weights = counts.astype(jnp.float32)
    member_share = weights[lax.axis_index("member")] / jnp.sum(weights)
    weighted = member_share * masses
    mixed = lax.psum(weighted, "member")
    running = congestion(kernel, mixed)
    values = value_init
    for repeat in range(2):
        widened = extended(values, (("gx", 1), ("gy", 2)), 1)
        values = best_reply(widened, opened, running, absorb)
    return (masses[None], values)


def solution(mesh):
    placed = (
        P("member", None, "gx", "gy"),
        P("member", None, "gx", "gy"),
        P(None, "gx", "gy"),
        P("gx", "gy"),
        P(),
        P(),
    )
    return jax.shard_map(
        shards,
        mesh=mesh,
        in_specs=placed,
        out_specs=(P("member", None, "gx", "gy"), P(None, "gx", "gy")),
        check_vma=False,
    )
```

profile of v0, /device:TPU:32, one launch (start us, length us, event | category | flops | bytes accessed | tf_op | source)
XLA Modules:
  0.0 333.3 jit_solution(6878188033969745545)
XLA Ops:
  7.2 1.9 copy.120
  9.2 1.9 collective-permute-start.5
  11.1 2.4 collective-permute-start.4
  13.6 7.0 %collective-permute-start.1 = (f32[2,1,128]{2,1,0:T(1,128)S(1)}, f32[2,1,128]{2,1,0:T(1,128)S(1)}, u32[]{:S(2)}, u32[]{:S(2)}) collective-permute-start(f32[2,1,128]{2,1,0:T(1,128)S(1)} %get-tuple-element.43), channel_id=1, source_target_pairs={{4,0},{8,4},{12,8},{16,12},{20,16},{24,20},{28,24},{5,1},{9,5},{13... | collective-permute-start | bytes 3080 | tf_op jit(solution)/shard_map/ppermute | solution.py:20
  20.6 2.1 collective-permute-start
  23.3 1.9 collective-permute-start.13
  30.2 4.5 %collective-permute-start.2 = (f32[2,34,1]{2,1,0:T(8,128)S(1)}, f32[2,34,1]{2,1,0:T(8,128)S(1)}, u32[]{:S(2)}, u32[]{:S(2)}) collective-permute-start(f32[2,34,1]{2,1,0:T(8,128)S(1)} %get-tuple-element.40), channel_id=1, source_target_pairs={{0,1},{1,2},{2,3},{4,5},{5,6},{6,7},{8,9},{9,10},{10,11},{12,13},{... | collective-permute-start | bytes 824 | tf_op jit(solution)/shard_map/ppermute | solution.py:17
  36.0 3.1 collective-permute-start.12
  40.7 1.6 copy.48
  44.1 4.6 %collective-permute-start.6 = (f32[64,34,1]{0,2,1:T(1,128)S(1)}, f32[64,34,1]{0,2,1:T(1,128)S(1)}, u32[]{:S(2)}, u32[]{:S(2)}) collective-permute-start(f32[64,34,1]{0,2,1:T(1,128)S(1)} %copy.46), channel_id=1, source_target_pairs={{0,1},{1,2},{2,3},{4,5},{5,6},{6,7},{8,9},{9,10},{10,11},{12,13},{... | collective-permute-start | bytes 26120 | tf_op jit(solution)/shard_map/ppermute | solution.py:17
  51.6 4.4 %fusion.14 = (f32[64,32,128]{2,0,1:T(8,128)}, f32[64,32,128]{2,0,1:T(8,128)S(1)}) fusion(bf16[1,64,32,128]{3,2,1,0:T(8,128)(2,1)S(1)} %copy-done.1, f32[32,128]{1,0:T(8,128)S(1)} %convert_subtract_fusion, f32[64,32,128]{2,0,1:T(8,128)S(1)} %bitcast.127, f32[1,32,128]{2,0,1:T(1,128)S(1)} %slice.249, f32[63,32,128]{2,0,1:T(8,128)} %slice.248, ...), kind=kLoop, calls=%fused_computation.43 | loop fusion | flops 11010048 | bytes 5933056 | tf_op jit(solution)/shard_map/mul | solution.py:67
  56.1 2.4 collective-permute-start.9
  58.5 1.9 collective-permute-start.8
  60.4 3.3 collective-permute-done.8
  63.8 1.8 fusion.75
  65.6 1.6 copy.53
  68.5 1.6 copy.51
  70.1 4.7 %collective-permute-start.10 = (f32[64,34,1]{0,2,1:T(1,128)S(1)}, f32[64,34,1]{0,2,1:T(1,128)S(1)}, u32[]{:S(2)}, u32[]{:S(2)}) collective-permute-start(f32[64,34,1]{0,2,1:T(1,128)S(1)} %copy.51), channel_id=1, source_target_pairs={{0,1},{1,2},{2,3},{4,5},{5,6},{6,7},{8,9},{9,10},{10,11},{12,13},{... | collective-permute-start | bytes 26120 | tf_op jit(solution)/shard_map/ppermute | solution.py:17
  79.3 4.4 %multiply_bitcast_fusion = (f32[32,8,8,128]{3,2,1,0:T(8,128)S(1)}, f32[64,32,128]{2,0,1:T(8,128)}) fusion(f32[]{:T(128)S(6)} %div.17, f32[32,128]{1,0:T(8,128)S(1)} %convert_subtract_fusion, f32[64,32,128]{2,0,1:T(8,128)S(1)} %get-tuple-element.15, bf16[1,64,32,128]{3,2,1,0:T(8,128)(2,1)S(1)} %copy-done.1, f32[1,32,128]{2,0,1:T(1,128)S(1)} %slice.257, ...), kind=kLoop, calls=%fused_computation.119 | loop fusion | flops 11010048 | bytes 5933060
  87.4 1.6 copy.67
  89.0 3.6 %collective-permute-start.15 = (f32[64,34,1]{0,2,1:T(1,128)S(1)}, f32[64,34,1]{0,2,1:T(1,128)S(1)}, u32[]{:S(2)}, u32[]{:S(2)}) collective-permute-start(f32[64,34,1]{0,2,1:T(1,128)S(1)} %copy.67), channel_id=1, source_target_pairs={{0,1},{1,2},{2,3},{4,5},{5,6},{6,7},{8,9},{9,10},{10,11},{12,13},{... | collective-permute-start | bytes 26120 | tf_op jit(solution)/shard_map/ppermute | solution.py:17
  96.0 2.7 collective-permute-done.14
  100.1 3.5 %fusion.70 = (f32[32,128]{1,0:T(8,128)S(1)}, f32[64,32,128]{2,0,1:T(8,128)}) fusion(f32[64,32,128]{2,0,1:T(8,128)S(1)} %copy-done.3, f32[64,34,128]{2,0,1:T(8,128)S(1)} %constant_dynamic-update-slice_fusion, f32[64,34,1]{2,0,1:T(8,128)} %copy.68, f32[32,128]{1,0:T(8,128)S(1)} %get-tuple-element.39, f32[64]{0:T(128)S(1)} %get-tuple-element.45, ...), kind=kLoop, calls=%fused_computation.164 | loop fusion | flops 5500928 | bytes 3377152 | tf_op jit(solution)/shard_map/reduce_min | solution.py:84
  103.6 191.8 %all-reduce.2.cloned.1.call-done = f32[64,4096]{1,0:T(8,128)} async-done(((f32[64,4096]{1,0:T(8,128)}), f32[64,4096]{1,0:T(8,128)}) %all-reduce.2.cloned.1.call-update) | async-done | bytes 1048592 | tf_op jit(solution)/shard_map/psum | solution.py:114
  295.4 2.3 fusion.1
  299.2 1.9 collective-permute-start.16
  301.2 2.4 collective-permute-start.17
  303.6 2.8 collective-permute-done.17
  308.0 1.6 copy.75
  309.6 4.0 %collective-permute-start.19 = (f32[64,34,1]{0,2,1:T(1,128)S(1)}, f32[64,34,1]{0,2,1:T(1,128)S(1)}, u32[]{:S(2)}, u32[]{:S(2)}) collective-permute-start(f32[64,34,1]{0,2,1:T(1,128)S(1)} %copy.75), channel_id=1, source_target_pairs={{0,1},{1,2},{2,3},{4,5},{5,6},{6,7},{8,9},{9,10},{10,11},{12,13},{... | collective-permute-start | bytes 26120 | tf_op jit(solution)/shard_map/ppermute | solution.py:17
  315.3 2.8 copy.80
  321.1 2.3 fusion.67
  (100 shorter events, 36.9 us)
Async XLA Ops:
  7.2 288.2 %copy-start = (f32[64,64]{1,0:T(8,128)S(1)}, f32[64,64]{1,0:T(8,128)}, u32[]{:S(2)}) copy-start(f32[64,64]{1,0:T(8,128)} %param.11) | copy-start | bytes 49156
  7.2 6.3 %copy-start.11 = (s32[32,128]{1,0:T(8,128)S(1)}, s32[32,128]{1,0:T(8,128)}, u32[]{:S(2)}) copy-start(s32[32,128]{1,0:T(8,128)} %param.9) | copy-start | bytes 49156
  7.2 15.5 %copy-start.9 = (f32[64,32,128]{2,1,0:T(8,128)S(1)}, f32[64,32,128]{2,1,0:T(8,128)}, u32[]{:S(2)}) copy-start(f32[64,32,128]{2,1,0:T(8,128)} %param.8) | copy-start | bytes 3145732
  7.2 288.2 %all-reduce.2.cloned.1.call-start = ((), (), s32[]{:S(2)}) async-start(), calls=%async_computation | async-start | bytes 2097152 | tf_op jit(solution)/shard_map/psum | solution.py:114
  9.2 30.0 %collective-permute-start.5 = (f32[64,1,128]{2,0,1:T(8,128)S(1)}, f32[64,1,128]{2,0,1:T(8,128)S(1)}, u32[]{:S(2)}, u32[]{:S(2)}) collective-permute-start(f32[64,1,128]{2,0,1:T(8,128)S(1)} %get-tuple-element.35), channel_id=1, source_target_pairs={{4,0},{8,4},{12,8},{16,12},{20,16},{24,20},{28,24},{5,1},{9,5},{13... | collective-permute-start | bytes 98312 | tf_op jit(solution)/shard_map/ppermute | solution.py:20
  11.1 28.1 %collective-permute-start.4 = (f32[64,1,128]{2,0,1:T(8,128)S(1)}, f32[64,1,128]{2,0,1:T(8,128)S(1)}, u32[]{:S(2)}, u32[]{:S(2)}) collective-permute-start(f32[64,1,128]{2,0,1:T(8,128)S(1)} %get-tuple-element.34), channel_id=1, source_target_pairs={{0,4},{4,8},{8,12},{12,16},{16,20},{20,24},{24,28},{1,5},{5,9},{9,... | collective-permute-start | bytes 98312 | tf_op jit(solution)/shard_map/ppermute | solution.py:17
  13.6 14.6 %collective-permute-start.1 = (f32[2,1,128]{2,1,0:T(1,128)S(1)}, f32[2,1,128]{2,1,0:T(1,128)S(1)}, u32[]{:S(2)}, u32[]{:S(2)}) collective-permute-start(f32[2,1,128]{2,1,0:T(1,128)S(1)} %get-tuple-element.43), channel_id=1, source_target_pairs={{4,0},{8,4},{12,8},{16,12},{20,16},{24,20},{28,24},{5,1},{9,5},{13... | collective-permute-start | bytes 3080 | tf_op jit(solution)/shard_map/ppermute | solution.py:20
  20.6 4.7 %copy-start.12 = (s32[16]{0:T(128)S(1)}, s32[16]{0:T(128)}, u32[]{:S(2)}) copy-start(s32[16]{0:T(128)} %param.10) | copy-start | bytes 196
  20.6 5.3 %copy-start.1 = (bf16[1,64,32,128]{3,2,1,0:T(8,128)(2,1)S(1)}, bf16[1,64,32,128]{3,2,1,0:T(8,128)(2,1)}, u32[]{:S(2)}) copy-start(bf16[1,64,32,128]{3,2,1,0:T(8,128)(2,1)} %param.7) | copy-start | bytes 1572868
  20.6 5.3 %copy-start.7 = (f32[1,64,32,128]{3,2,1,0:T(8,128)S(1)}, f32[1,64,32,128]{3,2,1,0:T(8,128)}, u32[]{:S(2)}) copy-start(f32[1,64,32,128]{3,2,1,0:T(8,128)} %param.6) | copy-start | bytes 3145732
  20.6 7.5 %collective-permute-start = (f32[2,1,128]{2,1,0:T(1,128)S(1)}, f32[2,1,128]{2,1,0:T(1,128)S(1)}, u32[]{:S(2)}, u32[]{:S(2)}) collective-permute-start(f32[2,1,128]{2,1,0:T(1,128)S(1)} %get-tuple-element.42), channel_id=1, source_target_pairs={{0,4},{4,8},{8,12},{12,16},{16,20},{20,24},{24,28},{1,5},{5,9},{9,... | collective-permute-start | bytes 3080 | tf_op jit(solution)/shard_map/ppermute | solution.py:17
  23.3 3.5 %copy-start.2 = (f32[64,32,128]{2,0,1:T(8,128)}, f32[64,32,128]{2,0,1:T(8,128)S(1)}, u32[]{:S(2)}) copy-start(f32[64,32,128]{2,0,1:T(8,128)S(1)} %copy.59) | copy-start | bytes 3145732
  23.3 37.1 %collective-permute-start.13 = (f32[64,1,128]{2,0,1:T(8,128)S(1)}, f32[64,1,128]{2,0,1:T(8,128)S(1)}, u32[]{:S(2)}, u32[]{:S(2)}) collective-permute-start(f32[64,1,128]{2,0,1:T(8,128)S(1)} %get-tuple-element.31), channel_id=1, source_target_pairs={{0,4},{4,8},{8,12},{12,16},{16,20},{20,24},{24,28},{1,5},{5,9},{9,... | collective-permute-start | bytes 98312 | tf_op jit(solution)/shard_map/ppermute | solution.py:17
  28.2 7.7 %collective-permute-start.3 = (f32[2,34,1]{2,1,0:T(8,128)S(1)}, f32[2,34,1]{2,1,0:T(8,128)S(1)}, u32[]{:S(2)}, u32[]{:S(2)}) collective-permute-start(f32[2,34,1]{2,1,0:T(8,128)S(1)} %get-tuple-element.41), channel_id=1, source_target_pairs={{1,0},{2,1},{3,2},{5,4},{6,5},{7,6},{9,8},{10,9},{11,10},{13,12},{... | collective-permute-start | bytes 824 | tf_op jit(solution)/shard_map/ppermute | solution.py:20
  30.2 8.9 %collective-permute-start.2 = (f32[2,34,1]{2,1,0:T(8,128)S(1)}, f32[2,34,1]{2,1,0:T(8,128)S(1)}, u32[]{:S(2)}, u32[]{:S(2)}) collective-permute-start(f32[2,34,1]{2,1,0:T(8,128)S(1)} %get-tuple-element.40), channel_id=1, source_target_pairs={{0,1},{1,2},{2,3},{4,5},{5,6},{6,7},{8,9},{9,10},{10,11},{12,13},{... | collective-permute-start | bytes 824 | tf_op jit(solution)/shard_map/ppermute | solution.py:17
  36.0 49.9 %collective-permute-start.12 = (f32[64,1,128]{2,0,1:T(8,128)S(1)}, f32[64,1,128]{2,0,1:T(8,128)S(1)}, u32[]{:S(2)}, u32[]{:S(2)}) collective-permute-start(f32[64,1,128]{2,0,1:T(8,128)S(1)} %get-tuple-element.30), channel_id=1, source_target_pairs={{4,0},{8,4},{12,8},{16,12},{20,16},{24,20},{28,24},{5,1},{9,5},{13... | collective-permute-start | bytes 98312 | tf_op jit(solution)/shard_map/ppermute | solution.py:20
  42.4 6.3 %collective-permute-start.7 = (f32[64,34,1]{0,2,1:T(1,128)S(1)}, f32[64,34,1]{0,2,1:T(1,128)S(1)}, u32[]{:S(2)}, u32[]{:S(2)}) collective-permute-start(f32[64,34,1]{0,2,1:T(1,128)S(1)} %copy.48), channel_id=1, source_target_pairs={{1,0},{2,1},{3,2},{5,4},{6,5},{7,6},{9,8},{10,9},{11,10},{13,12},{... | collective-permute-start | bytes 26120 | tf_op jit(solution)/shard_map/ppermute | solution.py:20
  44.1 6.1 %collective-permute-start.6 = (f32[64,34,1]{0,2,1:T(1,128)S(1)}, f32[64,34,1]{0,2,1:T(1,128)S(1)}, u32[]{:S(2)}, u32[]{:S(2)}) collective-permute-start(f32[64,34,1]{0,2,1:T(1,128)S(1)} %copy.46), channel_id=1, source_target_pairs={{0,1},{1,2},{2,3},{4,5},{5,6},{6,7},{8,9},{9,10},{10,11},{12,13},{... | collective-permute-start | bytes 26120 | tf_op jit(solution)/shard_map/ppermute | solution.py:17
  56.1 4.4 %collective-permute-start.9 = (f32[64,1,128]{2,0,1:T(8,128)S(1)}, f32[64,1,128]{2,0,1:T(8,128)S(1)}, u32[]{:S(2)}, u32[]{:S(2)}) collective-permute-start(f32[64,1,128]{2,0,1:T(8,128)S(1)} %get-tuple-element.33), channel_id=1, source_target_pairs={{4,0},{8,4},{12,8},{16,12},{20,16},{24,20},{28,24},{5,1},{9,5},{13... | collective-permute-start | bytes 98312 | tf_op jit(solution)/shard_map/ppermute | solution.py:20
  58.5 5.2 %collective-permute-start.8 = (f32[64,1,128]{2,0,1:T(8,128)S(1)}, f32[64,1,128]{2,0,1:T(8,128)S(1)}, u32[]{:S(2)}, u32[]{:S(2)}) collective-permute-start(f32[64,1,128]{2,0,1:T(8,128)S(1)} %get-tuple-element.32), channel_id=1, source_target_pairs={{0,4},{4,8},{8,12},{12,16},{16,20},{20,24},{24,28},{1,5},{5,9},{9,... | collective-permute-start | bytes 98312 | tf_op jit(solution)/shard_map/ppermute | solution.py:17
  67.2 9.2 %collective-permute-start.11 = (f32[64,34,1]{0,2,1:T(1,128)S(1)}, f32[64,34,1]{0,2,1:T(1,128)S(1)}, u32[]{:S(2)}, u32[]{:S(2)}) collective-permute-start(f32[64,34,1]{0,2,1:T(1,128)S(1)} %copy.53), channel_id=1, source_target_pairs={{1,0},{2,1},{3,2},{5,4},{6,5},{7,6},{9,8},{10,9},{11,10},{13,12},{... | collective-permute-start | bytes 26120 | tf_op jit(solution)/shard_map/ppermute | solution.py:20
  70.1 5.0 %copy-start.6 = (f32[64,32,128]{2,0,1:T(8,128)S(1)}, f32[64,32,128]{2,0,1:T(8,128)}, u32[]{:S(2)}) copy-start(f32[64,32,128]{2,0,1:T(8,128)} %get-tuple-element.14) | copy-start | bytes 3145732
  70.1 7.8 %collective-permute-start.10 = (f32[64,34,1]{0,2,1:T(1,128)S(1)}, f32[64,34,1]{0,2,1:T(1,128)S(1)}, u32[]{:S(2)}, u32[]{:S(2)}) collective-permute-start(f32[64,34,1]{0,2,1:T(1,128)S(1)} %copy.51), channel_id=1, source_target_pairs={{0,1},{1,2},{2,3},{4,5},{5,6},{6,7},{8,9},{9,10},{10,11},{12,13},{... | collective-permute-start | bytes 26120 | tf_op jit(solution)/shard_map/ppermute | solution.py:17
  83.7 1.6 copy-start.10
  89.0 5.5 %collective-permute-start.15 = (f32[64,34,1]{0,2,1:T(1,128)S(1)}, f32[64,34,1]{0,2,1:T(1,128)S(1)}, u32[]{:S(2)}, u32[]{:S(2)}) collective-permute-start(f32[64,34,1]{0,2,1:T(1,128)S(1)} %copy.67), channel_id=1, source_target_pairs={{0,1},{1,2},{2,3},{4,5},{5,6},{6,7},{8,9},{9,10},{10,11},{12,13},{... | collective-permute-start | bytes 26120 | tf_op jit(solution)/shard_map/ppermute | solution.py:17
  93.0 5.6 %collective-permute-start.14 = (f32[64,34,1]{0,2,1:T(1,128)S(1)}, f32[64,34,1]{0,2,1:T(1,128)S(1)}, u32[]{:S(2)}, u32[]{:S(2)}) collective-permute-start(f32[64,34,1]{0,2,1:T(1,128)S(1)} %copy.64), channel_id=1, source_target_pairs={{1,0},{2,1},{3,2},{5,4},{6,5},{7,6},{9,8},{10,9},{11,10},{13,12},{... | collective-permute-start | bytes 26120 | tf_op jit(solution)/shard_map/ppermute | solution.py:20
  94.5 5.6 %copy-start.3 = (f32[64,32,128]{2,0,1:T(8,128)S(1)}, f32[64,32,128]{2,0,1:T(8,128)}, u32[]{:S(2)}) copy-start(f32[64,32,128]{2,0,1:T(8,128)} %copy-done.2) | copy-start | bytes 3145732
  103.6 194.1 %copy-start.8 = (f32[64,32,128]{2,0,1:T(8,128)S(1)}, f32[64,32,128]{2,0,1:T(8,128)}, u32[]{:S(2)}) copy-start(f32[64,32,128]{2,0,1:T(8,128)} %get-tuple-element.13) | copy-start | bytes 3145732
  299.2 4.3 %collective-permute-start.16 = (f32[64,1,128]{2,0,1:T(8,128)S(1)}, f32[64,1,128]{2,0,1:T(8,128)S(1)}, u32[]{:S(2)}, u32[]{:S(2)}) collective-permute-start(f32[64,1,128]{2,0,1:T(8,128)S(1)} %get-tuple-element.29), channel_id=1, source_target_pairs={{4,0},{8,4},{12,8},{16,12},{20,16},{24,20},{28,24},{5,1},{9,5},{13... | collective-permute-start | bytes 98312 | tf_op jit(solution)/shard_map/ppermute | solution.py:20
  301.2 5.2 %collective-permute-start.17 = (f32[64,1,128]{2,0,1:T(8,128)S(1)}, f32[64,1,128]{2,0,1:T(8,128)S(1)}, u32[]{:S(2)}, u32[]{:S(2)}) collective-permute-start(f32[64,1,128]{2,0,1:T(8,128)S(1)} %get-tuple-element.28), channel_id=1, source_target_pairs={{0,4},{4,8},{8,12},{12,16},{16,20},{20,24},{24,28},{1,5},{5,9},{9,... | collective-permute-start | bytes 98312 | tf_op jit(solution)/shard_map/ppermute | solution.py:17
  309.6 8.5 %collective-permute-start.19 = (f32[64,34,1]{0,2,1:T(1,128)S(1)}, f32[64,34,1]{0,2,1:T(1,128)S(1)}, u32[]{:S(2)}, u32[]{:S(2)}) collective-permute-start(f32[64,34,1]{0,2,1:T(1,128)S(1)} %copy.75), channel_id=1, source_target_pairs={{0,1},{1,2},{2,3},{4,5},{5,6},{6,7},{8,9},{9,10},{10,11},{12,13},{... | collective-permute-start | bytes 26120 | tf_op jit(solution)/shard_map/ppermute | solution.py:17
  314.0 5.6 %collective-permute-start.18 = (f32[64,34,1]{0,2,1:T(1,128)S(1)}, f32[64,34,1]{0,2,1:T(1,128)S(1)}, u32[]{:S(2)}, u32[]{:S(2)}) collective-permute-start(f32[64,34,1]{0,2,1:T(1,128)S(1)} %copy.73), channel_id=1, source_target_pairs={{1,0},{2,1},{3,2},{5,4},{6,5},{7,6},{9,8},{10,9},{11,10},{13,12},{... | collective-permute-start | bytes 26120 | tf_op jit(solution)/shard_map/ppermute | solution.py:20
  (2 other events, 2.7 us)
Sparse Core Ops, SparseCore 0:
  84.9 210.4 all-reduce.1
where the time goes:
time: 335 us; the launch traced here: 333 us
  waiting for transfers between devices  202 us (60%)
  starting transfers between devices  55.1 us (16%)
  local copies, waits for them, and re-layouts  38.4 us (11%)
  other arithmetic  16.9 us (5%)
  between operations  15.9 us (5%)
  matrix products  5.24 us (2%)
    psum x1, waiting for transfers between devices, shards(): mixed = lax.psum(weighted, 'member')  192 us
    ppermute x10, starting transfers between devices, extended(): lax.ppermute(lax.slice_in_dim(block, block.shape[dim] - width, None, axis...  32.1 us
    ppermute x10, starting transfers between devices, extended(): lax.ppermute(lax.slice_in_dim(block, 0, width, axis=dim), axis, backward)  23 us
    slice x10, local copies, waits for them, and re-layouts, extended(): lax.slice_in_dim(block, block.shape[dim] - width, None, axis=dim)  8.54 us
    unnamed x32, local copies, waits for them, and re-layouts  8.23 us
    slice x7, local copies, waits for them, and re-layouts, extended(): lax.slice_in_dim(block, 0, width, axis=dim)  6.93 us
  transfers between devices with their start and end apart: 21, of which 5 were waited for; matrix products, arithmetic and copies ran while one was open for 13% of the time, Pallas kernels for 0%

commit v1 on v0

v1 whole, which is shorter than its diff:
```python
import jax
import jax.numpy as jnp
import numpy as np
from jax import lax
from jax.experimental import pallas as pl
from jax.experimental.pallas import tpu as pltpu
from jax.sharding import PartitionSpec as P

MESH = pl.DeviceIdType.MESH
F32 = jnp.float32
BF16 = jnp.bfloat16
I16 = jnp.int16
I32 = jnp.int32

H, X, Y = 64, 32, 128
SPEED = 0.55
BOUND = 9.5

ROW_UP, ROW_DOWN, COL_UP, COL_DOWN, VAL_UP, VAL_DOWN = range(6)
STEP_ROW, STEP_COL, OVER_Y, OVER_Z, REPLY, GATHER = 6, 10, 14, 26, 34, 38
COPIES = 44


def tables():
    angles = np.arange(H, dtype=np.float32) * np.float32(2.0 * np.pi / H)
    along_x = np.abs(SPEED * np.cos(angles)).astype(np.float32)
    along_y = np.abs(SPEED * np.sin(angles)).astype(np.float32)
    spread = angles[:, None] - angles[None, :]
    coupling = np.exp(-5.0 * (1.0 - np.cos(spread.astype(np.float64)))).astype(np.float32)
    wide = lambda v: np.ascontiguousarray(np.broadcast_to(v[:, None], (H, Y)))
    return wide(along_x), wide(along_y), coupling


def encode(x):
    root = jnp.sqrt(jnp.maximum(x, 0.0)) * 65535.0 + 0.5
    return (root.astype(I32) - 32768).astype(I16)


def decode(code):
    root = code.astype(I32).astype(F32) + 32768.0
    return root * root * (BOUND / (65535.0 * 65535.0))


def split_left(m):
    high = m.astype(BF16)
    low = (m - high.astype(F32)).astype(BF16)
    return high, low


def widen(m):
    high, low = split_left(m)
    return jnp.concatenate([high, low, high, low], axis=0)


def kernel(
    counts, density, turn_hbm, value_hbm, labels_hbm, ax_hbm, ay_hbm, coupling_hbm, kernel_hbm,
    moved, values,
    r0, turn, val, labels, axt, ayt, coupling, kern,
    sx_m, sx_p, sy_m, sy_p, sv_m, sv_p, hx_m, hx_p, hy_m, hy_p, hv_m, hv_p,
    r1, r2, s2x, s2y, h2x, h2y, weights, keep,
    ysend, yrecv, zsend, zrecv, total, base,
    up_row, down_row, cs, kf, cf,
    sr_m, sr_p, sc_m, sc_p, hr_m, hr_p, hc_m, hc_p,
    gsend, grecv, out,
    load_sem, out_sem, ss, rs,
):
    member = lax.axis_index("member")
    gx = lax.axis_index("gx")
    gy = lax.axis_index("gy")
    zh, y = member // 4, member % 4
    odd = gx % 2
    q = jnp.where(odd == 1, 3 - y, y)
    turn_sign = jnp.where(odd == 1, 3, 1)

    def at(z, yy):
        return {"member": z * 4 + yy}

    pair = (jnp.where(zh % 2 == 0, zh + 1, zh - 1), 3 - zh)

    barrier = pltpu.get_barrier_semaphore()
    greeted = [at(zh, (y + d) % 4) for d in (1, 2, 3)] + [at(p, y) for p in pair]
    greeted += [{"gx": (gx + d) % 8} for d in (1, 7)] + [{"gy": (gy + d) % 4} for d in (1, 3)]
    for target in greeted:
        pl.semaphore_signal(barrier, inc=1, device_id=target, device_id_type=MESH)

    loads = [
        pltpu.make_async_copy(src, dst, load_sem.at[i])
        for i, (src, dst) in enumerate((
            (density, r0), (labels_hbm, labels), (value_hbm, val), (turn_hbm, turn), (ax_hbm, axt), (ay_hbm, ayt),
            (coupling_hbm, coupling), (kernel_hbm, kern),
        ))
    ]
    for c in loads:
        c.start()

    def copy(i, src, dst, target):
        return pltpu.make_async_remote_copy(
            src_ref=src, dst_ref=dst, send_sem=ss.at[i], recv_sem=rs.at[i], device_id=target, device_id_type=MESH
        )

    has_m, has_p = gx > 0, gx < 7
    west, east = gy > 0, gy < 3
    to_m, to_p = {"gx": (gx + 7) % 8}, {"gx": (gx + 1) % 8}
    to_w, to_e = {"gy": (gy + 3) % 4}, {"gy": (gy + 1) % 4}
    lane = lax.broadcasted_iota(I32, (X, Y), 1)
    row = lax.broadcasted_iota(I32, (X, Y), 0)
    lane_h = lax.broadcasted_iota(I32, (32, Y), 1)

    def shift_x(r, halo, k):
        if k in (0, 3):
            return jnp.where(row == 0, halo, pltpu.roll(r, 1, 0))
        return jnp.where(row == X - 1, halo, pltpu.roll(r, X - 1, 0))

    def shift_y(r, halo, position, k):
        if k in (0, 1):
            moved_halo = pltpu.roll(halo, lax.rem(Y - position, Y), 1)
            return jnp.where(lane == 0, moved_halo, pltpu.roll(r, 1, 1))
        moved_halo = pltpu.roll(halo, Y - 1 - position, 1)
        return jnp.where(lane == Y - 1, moved_halo, pltpu.roll(r, Y - 1, 1))

    def pack_column(acc, r, position, k):
        shift = position + 1 if k in (0, 1) else position
        return jnp.where(lane == position, pltpu.roll(r, shift, 1), acc)

    loads[0].wait()
    loads[1].wait()
    opened = jnp.where(labels[...] != 1, 1.0, 0.0).astype(F32)
    keep[...] = jnp.where(labels[...] == 2, 0.0, 1.0).astype(F32)
    zero_plane = jnp.zeros((X, Y), F32)

    def rows_of(ref, h0, n, x):
        return ref.reshape(H * X, Y)[pl.ds(h0 * X + x, n, stride=X), :]

    sx_p[0:16, :] = rows_of(r0, 0, 16, X - 1)
    sx_p[16:32, :] = rows_of(r0, 48, 16, X - 1)
    sx_p[32:40, :] = jnp.broadcast_to(opened[X - 1:X, :], (8, Y))
    sx_m[0:32, :] = rows_of(r0, 16, 32, 0)
    sx_m[32:40, :] = jnp.broadcast_to(opened[0:1, :], (8, Y))

    for k0, dst, shift in ((0, sy_p, 65), (2, sy_m, 64)):
        def pack(j, acc, k0=k0):
            return pack_column(acc, r0[k0 * 16 + j], j, k0)
        acc = lax.fori_loop(0, 32, pack, zero_plane, unroll=4)
        dst[0:32, :] = jnp.where(lane == 64, pltpu.roll(opened, shift, 1), acc)

    def value_row(i):
        return val.reshape(H * X, Y)[pl.ds(q * 8 + i, H, stride=X), :]

    def pack_values(rows, headings, side):
        acc = jnp.zeros((32, Y), F32)
        for i in range(8):
            part = rows[i][headings:headings + 32, :]
            shift = i + 1 if side else i
            acc = jnp.where(lane_h == i, pltpu.roll(part, shift, 1) if shift else part, acc)
        return acc

    loads[2].wait()
    own = [value_row(i) for i in range(8)]
    sy_p[32:64, :] = pack_values(own, 32, True)
    sy_m[32:64, :] = pack_values(own, 0, False)
    sv_p[...] = own[7][16:48, :]
    sv_m[0:16, :] = own[0][0:16, :]
    sv_m[16:32, :] = own[0][48:64, :]

    @pl.when(gx == 0)
    def _():
        hx_m[...] = jnp.zeros((40, Y), F32)
        hv_m[...] = jnp.zeros((32, Y), F32)
        h2x[0] = jnp.zeros((16, Y), F32)
        h2x[3] = jnp.zeros((16, Y), F32)

    @pl.when(gx == 7)
    def _():
        hx_p[...] = jnp.zeros((40, Y), F32)
        hv_p[...] = jnp.zeros((32, Y), F32)
        h2x[1] = jnp.zeros((16, Y), F32)
        h2x[2] = jnp.zeros((16, Y), F32)

    @pl.when(gy == 0)
    def _():
        hy_m[...] = jnp.zeros((64, Y), F32)
        hc_m[...] = jnp.zeros((32, Y), F32)
        h2y[0] = zero_plane
        h2y[1] = zero_plane

    @pl.when(gy == 3)
    def _():
        hy_p[...] = jnp.zeros((64, Y), F32)
        hc_p[...] = jnp.zeros((32, Y), F32)
        h2y[2] = zero_plane
        h2y[3] = zero_plane

    low, high = q == 0, q == 3
    near_up = {"member": zh * 4 + jnp.where(low, y, (y + 4 - turn_sign) % 4), "gx": jnp.where(low, (gx + 7) % 8, gx)}
    near_down = {"member": zh * 4 + jnp.where(high, y, (y + turn_sign) % 4), "gx": jnp.where(high, (gx + 1) % 8, gx)}
    has_up, has_down = jnp.logical_or(q > 0, has_m), jnp.logical_or(q < 3, has_p)

    @pl.when(jnp.logical_not(has_up))
    def _():
        hr_m[...] = jnp.zeros((32, Y), F32)

    @pl.when(jnp.logical_not(has_down))
    def _():
        hr_p[...] = jnp.zeros((32, Y), F32)

    first = (
        (copy(ROW_DOWN, sx_p, hx_m, to_p), has_p, has_m),
        (copy(ROW_UP, sx_m, hx_p, to_m), has_m, has_p),
        (copy(COL_DOWN, sy_p, hy_m, to_e), east, west),
        (copy(COL_UP, sy_m, hy_p, to_w), west, east),
        (copy(VAL_DOWN, sv_p, hv_m, to_p), jnp.logical_and(high, has_p), jnp.logical_and(low, has_m)),
        (copy(VAL_UP, sv_m, hv_p, to_m), jnp.logical_and(low, has_m), jnp.logical_and(high, has_p)),
    )

    def start(c, condition):
        @pl.when(condition)
        def _():
            c.start()

    def wait_recv(c, condition):
        @pl.when(condition)
        def _():
            c.wait_recv()

    def wait_send(c, condition):
        @pl.when(condition)
        def _():
            c.wait_send()

    pl.semaphore_wait(barrier, len(greeted))
    for c, sends, _ in first:
        start(c, sends)
    for c in loads[3:]:
        c.wait()
    kf[:, 0:64] = kern[...]
    kf[:, 64:128] = kern[...]
    for c, _, receives in first[:4]:
        wait_recv(c, receives)

    open_p = jnp.where(row == X - 1, hx_p[32:33, :], pltpu.roll(opened, X - 1, 0))
    open_m = jnp.where(row == 0, hx_m[32:33, :], pltpu.roll(opened, 1, 0))
    open_e = jnp.where(lane == Y - 1, pltpu.roll(hy_p[0:32, :], 63, 1), pltpu.roll(opened, Y - 1, 1))
    open_w = jnp.where(lane == 0, pltpu.roll(hy_m[0:32, :], 64, 1), pltpu.roll(opened, 1, 1))
    weights[0] = opened * open_p
    weights[1] = opened * open_m
    weights[2] = opened * open_e
    weights[3] = opened * open_w

    def transport(k, src, dst, halo_x, x_at, halo_y, y_at, pack):
        out_x, in_x = (0, 1) if k in (0, 3) else (1, 0)
        out_y, in_y = (2, 3) if k in (0, 1) else (3, 2)
        wox, wix, woy, wiy = weights[out_x], weights[in_x], weights[out_y], weights[in_y]
        kept = keep[...]
        columns = halo_y[0:32, :] if y_at is not None else halo_y[k]
        h0 = 16 * k
        y_from = 0 if y_at is None else y_at

        def turns(h):
            r = src[h]
            t = turn[h].astype(F32)
            up = jnp.maximum(t, 0.0) * r
            return r, up, up - t * r

        def start_of(j):
            h = h0 + j
            r, up, down = turns(h)
            ax = axt[pl.ds(h, 1), :]
            ay = ayt[pl.ds(h, 1), :]
            hx = halo_x[pl.ds(x_at + j, 1), :] if x_at is not None else halo_x[k, pl.ds(j, 1), :]
            xn = shift_x(r, hx, k)
            yn = shift_y(r, columns, y_from + j, k)
            s = r - up - down + ax * (wix * xn - wox * r) + ay * (wiy * yn - woy * r)
            return s, up, down

        _, up_before, _ = turns((h0 + 63) % 64)
        s, up, _ = start_of(0)
        carry = (s + up_before, up, zero_plane)

        def finish(j, partial, down, acc):
            new = (partial + down) * kept
            dst[h0 + j] = new
            return pack_column(acc, new, j, k) if pack else acc

        def body(j, carry):
            partial, up_last, acc = carry
            s, up, down = start_of(j)
            acc = finish(j - 1, partial, down, acc)
            return s + up_last, up, acc

        partial, _, acc = lax.fori_loop(1, 16, body, carry, unroll=3)
        _, _, down = turns((h0 + 16) % 64)
        return finish(15, partial, down, acc)

    second = []
    for k in range(4):
        halo_x, x_at = ((hx_m, 0), (hx_p, 0), (hx_p, 16), (hx_m, 16))[k]
        halo_y, y_at = ((hy_m, 0), (hy_m, 16), (hy_p, 0), (hy_p, 16))[k]
        acc = transport(k, r0, r1, halo_x, x_at, halo_y, y_at, True)
        s2y[k] = acc
        s2x[k] = rows_of(r1, 16 * k, 16, X - 1 if k in (0, 3) else 0)
        if k in (0, 3):
            rows = (copy(STEP_ROW + k, s2x.at[k], h2x.at[k], to_p), has_p, has_m)
        else:
            rows = (copy(STEP_ROW + k, s2x.at[k], h2x.at[k], to_m), has_m, has_p)
        if k in (0, 1):
            columns = (copy(STEP_COL + k, s2y.at[k], h2y.at[k], to_e), east, west)
        else:
            columns = (copy(STEP_COL + k, s2y.at[k], h2y.at[k], to_w), west, east)
        for c, sends, receives in (rows, columns):
            start(c, sends)
            second.append((c, sends, receives))

    over_y = [[], [], [], []]
    stores = []
    for k in range(4):
        for c, _, receives in second[2 * k:2 * k + 2]:
            wait_recv(c, receives)
        transport(k, r1, r2, h2x, None, h2y, None, False)
        block = pl.ds(16 * k, 16)
        c = pltpu.make_async_copy(r2.at[block], moved.at[block], out_sem.at[k])
        c.start()
        stores.append(c)
        for d in (2, 1, 3):
            yy = (y + d) % 4
            qq = jnp.where(odd == 1, 3 - yy, yy)
            part = r2[block, pl.ds(pl.multiple_of(qq * 8, 8), 8), :]
            ysend[k, d - 1] = encode(part.reshape(128, Y) * (1.0 / BOUND))
            c = copy(OVER_Y + 3 * k + d - 1, ysend.at[k, d - 1], yrecv.at[k, d - 1], at(zh, yy))
            c.start()
            over_y[k].append(c)

    def count(z, yy):
        return counts[z * 4 + yy].astype(F32)

    def plane_of(scalar):
        return jnp.full((8, Y), scalar, F32)

    def group(z):
        return count(z, 0) + count(z, 1) + count(z, 2) + count(z, 3)

    mine, across = group(zh), [group(p) for p in pair]
    everyone = group(0) + group(1) + group(2) + group(3)
    inverse_all = 1.0 / plane_of(everyone)
    inverse_mine = (1.0 / BOUND) / plane_of(mine)

    def scaled(part, factor):
        return (part.reshape(16, 8, Y) * factor).reshape(128, Y)

    over_z = [[None, None] for _ in range(4)]
    for k in range(4):
        block = pl.ds(16 * k, 16)
        part = r2[block, pl.ds(pl.multiple_of(q * 8, 8), 8), :].reshape(128, Y) * count(zh, y)
        for c, d in zip(over_y[k], (2, 1, 3)):
            c.wait_recv()
            part = part + decode(yrecv[k, d - 1]) * count(zh, (y + 4 - d) % 4)
        zsend[k, 0] = encode(scaled(part, inverse_mine))
        c = copy(OVER_Z + 2 * k, zsend.at[k, 0], zrecv.at[k, 0], at(pair[k % 2], y))
        c.start()
        over_z[k][0] = c

    wait_recv(first[4][0], first[4][2])
    wait_recv(first[5][0], first[5][2])

    @pl.when(low)
    def _():
        up_row[...] = hv_m[...]

    @pl.when(q > 0)
    def _():
        up_row[...] = val.reshape(H * X, Y)[pl.ds(16 * X + q * 8 - 1, 32, stride=X), :]

    @pl.when(high)
    def _():
        down_row[...] = hv_p[...]

    @pl.when(q < 3)
    def _():
        down_row[0:16, :] = val.reshape(H * X, Y)[pl.ds(q * 8 + 8, 16, stride=X), :]
        down_row[16:32, :] = val.reshape(H * X, Y)[pl.ds(48 * X + q * 8 + 8, 16, stride=X), :]

    wide_rows = pl.ds(pl.multiple_of(q * 8, 8), 8)
    w_rows = [weights[i, wide_rows, :] for i in range(4)]
    keep_rows = keep[wide_rows, :]
    kf_high, kf_low = split_left(kf[...])
    lane_c = lax.broadcasted_iota(I32, (64, 2 * Y), 1)
    kb = jnp.concatenate([kf_high, kf_low], axis=1)
    cf[:, 0:64] = coupling[...]
    cf[:, 64:128] = coupling[...]
    cf_high, cf_low = split_left(cf[...])
    cb = jnp.concatenate([cf_high, cf_low], axis=1)

    def reply(rows, before, after, first_column, last_column, indices):
        lowest_of, columns = [], []
        for i in indices:
            v = rows[i]
            prior = rows[i - 1][16:48, :] if i > 0 else before
            if i < 7:
                later = (rows[i + 1][0:16, :], rows[i + 1][48:64, :])
            else:
                later = (after[0:16, :], after[16:32, :])
            lane_of = lax.broadcasted_iota(I32, (32, Y), 1)
            north = jnp.where(lane_of == Y - 1, pltpu.roll(last_column, Y - 1 - i, 1), pltpu.roll(v[0:32, :], Y - 1, 1))
            west_column = pltpu.roll(first_column, Y - i, 1) if i else first_column
            south = jnp.where(lane_of == 0, west_column, pltpu.roll(v[32:64, :], 1, 1))
            moves = []
            for k in range(4):
                part = slice(16 * k, 16 * k + 16)
                vk = v[part, :]
                xn = (later[0], prior[0:16, :], prior[16:32, :], later[1])[k]
                yn = (north[0:16, :], north[16:32, :], south[0:16, :], south[16:32, :])[k]
                wx = w_rows[0 if k in (0, 3) else 1][i:i + 1, :]
                wy = w_rows[2 if k in (0, 1) else 3][i:i + 1, :]
                moves.append(vk + axt[part, :] * (wx * (xn - vk)) + ayt[part, :] * (wy * (yn - vk)))
            moves = jnp.concatenate(moves, axis=0)
            lowest = jnp.min(moves, axis=0, keepdims=True)
            lowest_of.append(lowest)
            columns.append(jnp.exp((lowest - moves) * 10.0))
        summed = jnp.dot(cb, widen(jnp.concatenate(columns, axis=1)), preferred_element_type=F32)
        logs = jnp.log(summed) * 0.1
        return [lowest_of[n] - logs[:, n * Y:(n + 1) * Y] for n in range(len(indices))]

    from_start = reply(own, up_row[...], down_row[...], hy_m[32:64, :], hy_p[32:64, :], range(8))
    for i in range(8):
        base[i] = from_start[i]

    lower = [jnp.full((8, Y), zh, I32) < jnp.full((8, Y), p, I32) for p in pair]

    def merge(k, stage, partner, weight_own, weight_other):
        a = decode(zsend[k, stage]).reshape(16, 8, Y) * weight_own
        b = decode(zrecv[k, stage]).reshape(16, 8, Y) * weight_other
        is_low = lower[partner]
        return jnp.where(is_low, a, b) + jnp.where(is_low, b, a)

    for k in range(4):
        p = k % 2
        over_z[k][0].wait_recv()
        both = merge(k, 0, p, mine, across[p])
        factor = (1.0 / BOUND) / plane_of(mine + across[p])
        zsend[k, 1] = encode((both * factor).reshape(128, Y))
        c = copy(OVER_Z + 2 * k + 1, zsend.at[k, 1], zrecv.at[k, 1], at(pair[1 - p], y))
        c.start()
        over_z[k][1] = c
    for k in range(4):
        p = k % 2
        over_z[k][1].wait_recv()
        here = mine + across[p]
        mixed = merge(k, 1, 1 - p, here, everyone - here) * inverse_all
        total[pl.ds(128 * k, 128), :] = mixed.reshape(128, Y)

    mixed_rows = jnp.concatenate([total[pl.ds(i, H, stride=8), :] for i in range(8)], axis=1)
    running = 0.5 + 0.5 * jnp.dot(kb, widen(mixed_rows), preferred_element_type=F32)
    cost = [running[:, i * Y:(i + 1) * Y] for i in range(8)]
    once = [(cost[i] + base[i]) * keep_rows[i:i + 1, :] for i in range(8)]

    sr_p[...] = once[7][16:48, :]
    sr_m[0:16, :] = once[0][0:16, :]
    sr_m[16:32, :] = once[0][48:64, :]
    sc_p[...] = pack_values(once, 32, True)
    sc_m[...] = pack_values(once, 0, False)
    edges = (
        (copy(REPLY, sr_p, hr_m, near_down), has_down, has_up),
        (copy(REPLY + 1, sr_m, hr_p, near_up), has_up, has_down),
        (copy(REPLY + 2, sc_p, hc_m, to_e), east, west),
        (copy(REPLY + 3, sc_m, hc_p, to_w), west, east),
    )
    for c, sends, _ in edges:
        start(c, sends)
    for c, _, receives in edges:
        wait_recv(c, receives)

    out_rows = out.reshape(H * X, Y)

    def unpack(codes, qq, half):
        scale = codes[256:257, :].astype(F32) * (0.125 / 32767.0)
        for n in range(4):
            v = codes[64 * n:64 * n + 64, :].astype(F32) * scale
            out_rows[pl.ds(qq * 8 + 4 * half + n, H, stride=X), :] = v

    gathers = []
    for half in range(2):
        indices = range(4 * half, 4 * half + 4)
        twice = reply(once, hr_m[...], hr_p[...], hc_m[...], hc_p[...], indices)
        twice = [(cost[i] + t) * keep_rows[i:i + 1, :] for i, t in zip(indices, twice)]
        top = jnp.max(jnp.abs(jnp.concatenate(twice, axis=0)), axis=0, keepdims=True)
        eighths = (top * 8.0).astype(I32) + 1
        inverse = (32767.0 * 8.0) / eighths.astype(F32)
        for n in range(4):
            code = (twice[n] * inverse + 32768.5).astype(I32) - 32768
            gsend[half, pl.ds(64 * n, 64), :] = code.astype(I16)
        gsend[half, pl.ds(256, 16), :] = jnp.broadcast_to(eighths, (16, Y)).astype(I16)
        for d in (2, 1, 3):
            c = copy(GATHER + 3 * half + d - 1, gsend.at[half], grecv.at[half, d - 1], at(zh, (y + d) % 4))
            c.start()
            gathers.append((c, half, d))
    for half in range(2):
        unpack(gsend[half].astype(I32), q, half)
    for c, half, d in gathers:
        c.wait_recv()
        yy = (y + 4 - d) % 4
        unpack(grecv[half, d - 1].astype(I32), jnp.where(odd == 1, 3 - yy, yy), half)
    c = pltpu.make_async_copy(out, values, out_sem.at[4])
    c.start()
    stores.append(c)

    for c, sends, _ in (*first, *second, *edges):
        wait_send(c, sends)
    for k in range(4):
        for c in (*over_y[k], *over_z[k]):
            c.wait_send()
    for c, _, _ in gathers:
        c.wait_send()
    for c in stores:
        c.wait()


def shards(density, turn_rate, value_init, labels, counts, kernel_matrix):
    along_x, along_y, coupling = tables()
    vmem = lambda *shape: pltpu.VMEM(shape, F32)
    anywhere = pl.BlockSpec(memory_space=pl.ANY)
    scratch = [
        vmem(H, X, Y), pltpu.VMEM((H, X, Y), BF16), vmem(H, X, Y), pltpu.VMEM((X, Y), I32), vmem(H, Y), vmem(H, Y),
        vmem(H, H), vmem(H, H),
        vmem(40, Y), vmem(40, Y), vmem(64, Y), vmem(64, Y), vmem(32, Y), vmem(32, Y),
        vmem(40, Y), vmem(40, Y), vmem(64, Y), vmem(64, Y), vmem(32, Y), vmem(32, Y),
        vmem(H, X, Y), vmem(H, X, Y), vmem(4, 16, Y), vmem(4, X, Y), vmem(4, 16, Y), vmem(4, X, Y), vmem(4, X, Y),
        vmem(X, Y),
        pltpu.VMEM((4, 3, 128, Y), I16), pltpu.VMEM((4, 3, 128, Y), I16),
        pltpu.VMEM((4, 2, 128, Y), I16), pltpu.VMEM((4, 2, 128, Y), I16), vmem(512, Y), vmem(8, H, Y),
        vmem(32, Y), vmem(32, Y), vmem(8, Y), vmem(H, 128), vmem(H, 128),
        *[vmem(32, Y) for _ in range(8)],
        pltpu.VMEM((2, 272, Y), I16), pltpu.VMEM((2, 3, 272, Y), I16), vmem(H, X, Y),
        pltpu.SemaphoreType.DMA((8,)), pltpu.SemaphoreType.DMA((5,)),
        pltpu.SemaphoreType.DMA((COPIES,)), pltpu.SemaphoreType.DMA((COPIES,)),
    ]
    moved, values = pl.pallas_call(
        kernel,
        out_shape=(jax.ShapeDtypeStruct((H, X, Y), F32), jax.ShapeDtypeStruct((H, X, Y), F32)),
        in_specs=[pl.BlockSpec(memory_space=pltpu.SMEM)] + [anywhere] * 8,
        out_specs=(anywhere, anywhere),
        scratch_shapes=scratch,
        compiler_params=pltpu.CompilerParams(
            collective_id=1, has_side_effects=True, vmem_limit_bytes=40 * 1024 * 1024
        ),
        name="play",
    )(
        counts, density[0], turn_rate[0], value_init, labels,
        jnp.asarray(along_x), jnp.asarray(along_y), jnp.asarray(coupling), kernel_matrix,
    )
    return moved[None], values


def solution(mesh):
    placed = (
        P("member", None, "gx", "gy"),
        P("member", None, "gx", "gy"),
        P(None, "gx", "gy"),
        P("gx", "gy"),
        P(),
        P(),
    )
    return jax.shard_map(
        shards,
        mesh=mesh,
        in_specs=placed,
        out_specs=(P("member", None, "gx", "gy"), P(None, "gx", "gy")),
        check_vma=False,
    )
```

time: 335 us -> 66.3 us (0.20)
  the two profiles are of different devices: /device:TPU:32 before, /device:TPU:10 now
where the time goes in v1:
time: 66.3 us; the launch traced here: 65.7 us
  Pallas kernels  55.2 us (83%)
  local copies, waits for them, and re-layouts  9.83 us (15%)
    pallas_call x1, Pallas kernels, shards(): pl.pallas_call(kernel, out_shape=(jax.ShapeDtypeStruct((H, X, Y), F32), j...  55.2 us
    unnamed x20, local copies, waits for them, and re-layouts  9.83 us

profile of v1, /device:TPU:10, one launch (start us, length us, event | category | flops | bytes accessed | tf_op | source)
XLA Modules:
  0.0 65.7 jit_solution(2863489534883367780)
XLA Ops:
  0.6 0.0 copy-start.8
  0.6 0.6 copy-done.8
  1.3 0.0 copy-start
  1.3 1.2 %copy-done = f32[1,64,32,128]{3,2,1,0:T(8,128)S(1)} copy-done((f32[1,64,32,128]{3,2,1,0:T(8,128)S(1)}, f32[1,64,32,128]{3,2,1,0:T(8,128)}, u32[]{:S(2)}) %copy-start) | copy-done | bytes 1048600
  2.5 0.0 copy-start.1
  2.5 1.2 %copy-done.1 = f32[64,32,128]{2,1,0:T(8,128)S(1)} copy-done((f32[64,32,128]{2,1,0:T(8,128)S(1)}, f32[64,32,128]{2,1,0:T(8,128)}, u32[]{:S(2)}) %copy-start.1) | copy-done | bytes 1048600
  3.7 0.0 copy-start.2
  3.7 1.0 %copy-done.2 = bf16[1,64,32,128]{3,2,1,0:T(8,128)(2,1)S(1)} copy-done((bf16[1,64,32,128]{3,2,1,0:T(8,128)(2,1)S(1)}, bf16[1,64,32,128]{3,2,1,0:T(8,128)(2,1)}, u32[]{:S(2)}) %copy-start.2) | copy-done | bytes 524312
  4.8 0.0 copy-start.3
  4.8 0.8 %copy-done.3 = f32[64,64]{1,0:T(8,128)S(1)} copy-done((f32[64,64]{1,0:T(8,128)S(1)}, f32[64,64]{1,0:T(8,128)}, u32[]{:S(2)}) %copy-start.3) | copy-done | bytes 16408
  5.5 0.0 copy-start.4
  5.5 0.8 %copy-done.4 = f32[64,64]{1,0:T(8,128)S(1)} copy-done((f32[64,64]{1,0:T(8,128)S(1)}, f32[64,64]{1,0:T(8,128)}, u32[]{:S(2)}) %copy-start.4) | copy-done | bytes 16408
  6.3 0.0 copy-start.5
  6.3 0.8 %copy-done.5 = f32[64,128]{1,0:T(8,128)S(1)} copy-done((f32[64,128]{1,0:T(8,128)S(1)}, f32[64,128]{1,0:T(8,128)}, u32[]{:S(2)}) %copy-start.5) | copy-done | bytes 32792
  7.1 0.0 copy-start.6
  7.1 0.8 %copy-done.6 = f32[64,128]{1,0:T(8,128)S(1)} copy-done((f32[64,128]{1,0:T(8,128)S(1)}, f32[64,128]{1,0:T(8,128)}, u32[]{:S(2)}) %copy-start.6) | copy-done | bytes 32792
  7.8 0.0 copy-start.7
  7.8 0.7 %copy-done.7 = s32[32,128]{1,0:T(8,128)S(1)} copy-done((s32[32,128]{1,0:T(8,128)S(1)}, s32[32,128]{1,0:T(8,128)}, u32[]{:S(2)}) %copy-start.7) | copy-done | bytes 16408
  8.5 55.2 %play.1 = (f32[64,32,128]{2,1,0:T(8,128)S(1)}, f32[64,32,128]{2,1,0:T(8,128)S(1)}) custom-call(s32[16]{0:T(128)S(1)} %copy-done.8, f32[64,32,128]{2,1,0:T(8,128)S(1)} %bitcast.3, bf16[64,32,128]{2,1,0:T(8,128)(2,1)S(1)} %bitcast.5, f32[64,32,128]{2,1,0:T(8,128)S(1)} %copy-done.1, s32[32,128]{1,0:T(8,128)S(1)} %copy-done.7, f32[64,128]{1,0:T(8,128)S(1)} %copy-done.6, ...), custom_call_target="tpu_custom_call" | custom-call | tf_op jit(solution)/shard_map/play/pallas_call | solution.py:535
  63.7 1.0 %copy.13 = f32[1,64,32,128]{3,2,1,0:T(8,128)} copy(f32[1,64,32,128]{3,2,1,0:T(8,128)S(1)} %bitcast.4) | data formatting | bytes 2097152
  64.7 1.0 %copy.14 = f32[64,32,128]{2,1,0:T(8,128)} copy(f32[64,32,128]{2,1,0:T(8,128)S(1)} %get-tuple-element.9) | data formatting | bytes 2097152
Async XLA Ops:
  0.6 0.7 copy-start.8
  1.3 1.2 %copy-start = (f32[1,64,32,128]{3,2,1,0:T(8,128)S(1)}, f32[1,64,32,128]{3,2,1,0:T(8,128)}, u32[]{:S(2)}) copy-start(f32[1,64,32,128]{3,2,1,0:T(8,128)} %param.9) | copy-start | bytes 3145732
  2.5 1.2 %copy-start.1 = (f32[64,32,128]{2,1,0:T(8,128)S(1)}, f32[64,32,128]{2,1,0:T(8,128)}, u32[]{:S(2)}) copy-start(f32[64,32,128]{2,1,0:T(8,128)} %value_hbm.1) | copy-start | bytes 3145732
  3.7 1.0 %copy-start.2 = (bf16[1,64,32,128]{3,2,1,0:T(8,128)(2,1)S(1)}, bf16[1,64,32,128]{3,2,1,0:T(8,128)(2,1)}, u32[]{:S(2)}) copy-start(bf16[1,64,32,128]{3,2,1,0:T(8,128)(2,1)} %param.10) | copy-start | bytes 1572868
  4.8 0.8 %copy-start.3 = (f32[64,64]{1,0:T(8,128)S(1)}, f32[64,64]{1,0:T(8,128)}, u32[]{:S(2)}) copy-start(f32[64,64]{1,0:T(8,128)} %kernel_hbm.1) | copy-start | bytes 49156
  5.5 0.8 %copy-start.4 = (f32[64,64]{1,0:T(8,128)S(1)}, f32[64,64]{1,0:T(8,128)}, u32[]{:S(2)}) copy-start(f32[64,64]{1,0:T(8,128)} %constant.8.clone.coupling_hbm) | copy-start | bytes 49156
  6.3 0.8 %copy-start.5 = (f32[64,128]{1,0:T(8,128)S(1)}, f32[64,128]{1,0:T(8,128)}, u32[]{:S(2)}) copy-start(f32[64,128]{1,0:T(8,128)} %constant.7.clone.ay_hbm) | copy-start | bytes 98308
  7.1 0.8 %copy-start.6 = (f32[64,128]{1,0:T(8,128)S(1)}, f32[64,128]{1,0:T(8,128)}, u32[]{:S(2)}) copy-start(f32[64,128]{1,0:T(8,128)} %constant.6.clone.ax_hbm) | copy-start | bytes 98308
  7.8 0.7 %copy-start.7 = (s32[32,128]{1,0:T(8,128)S(1)}, s32[32,128]{1,0:T(8,128)}, u32[]{:S(2)}) copy-start(s32[32,128]{1,0:T(8,128)} %labels_hbm.1) | copy-start | bytes 49156

commit v2 on v1

--- a/solution.py
+++ b/solution.py
@@ -17,8 +17,17 @@
 BOUND = 9.5
 
 ROW_UP, ROW_DOWN, COL_UP, COL_DOWN, VAL_UP, VAL_DOWN = range(6)
-STEP_ROW, STEP_COL, OVER_Y, OVER_Z, REPLY, GATHER = 6, 10, 14, 26, 34, 38
-COPIES = 44
+CHUNK = 8
+CHUNKS = H // CHUNK
+ROWS = 8 * CHUNK
+STEP_ROW, STEP_COL, OVER_Y = 6, 10, 14
+OVER_Z = OVER_Y + 3 * CHUNKS
+REPLY = OVER_Z + 2 * CHUNKS
+GATHER = REPLY + 4
+PIECES = 4
+SPAN = 8 // PIECES
+MARK = H * SPAN
+COPIES = GATHER + 3 * PIECES
 
 
 def tables():
@@ -53,16 +62,16 @@
 
 
 def kernel(
-    counts, density, turn_hbm, value_hbm, labels_hbm, ax_hbm, ay_hbm, coupling_hbm, kernel_hbm,
-    moved, values,
+    counts_hbm, density, turn_hbm, value_hbm, labels_hbm, ax_hbm, ay_hbm, coupling_hbm, kernel_hbm,
+    r2, out,
     r0, turn, val, labels, axt, ayt, coupling, kern,
     sx_m, sx_p, sy_m, sy_p, sv_m, sv_p, hx_m, hx_p, hy_m, hy_p, hv_m, hv_p,
-    r1, r2, s2x, s2y, h2x, h2y, weights, keep,
+    r1, s2x, s2y, h2x, h2y, weights, keep,
     ysend, yrecv, zsend, zrecv, total, base,
     up_row, down_row, cs, kf, cf,
     sr_m, sr_p, sc_m, sc_p, hr_m, hr_p, hc_m, hc_p,
-    gsend, grecv, out,
-    load_sem, out_sem, ss, rs,
+    gsend, grecv,
+    counts, load_sem, ss, rs,
 ):
     member = lax.axis_index("member")
     gx = lax.axis_index("gx")
@@ -79,15 +88,26 @@
 
     barrier = pltpu.get_barrier_semaphore()
     greeted = [at(zh, (y + d) % 4) for d in (1, 2, 3)] + [at(p, y) for p in pair]
-    greeted += [{"gx": (gx + d) % 8} for d in (1, 7)] + [{"gy": (gy + d) % 4} for d in (1, 3)]
+    greeted += [{"gy": (gy + d) % 4} for d in (1, 3)]
+
+    def greet(target):
+        pl.semaphore_signal(barrier, inc=1, device_id=target, device_id_type=MESH)
+
+    has_m, has_p = gx > 0, gx < 7
+    west, east = gy > 0, gy < 3
+    to_m, to_p = {"gx": (gx + 7) % 8}, {"gx": (gx + 1) % 8}
+    to_w, to_e = {"gy": (gy + 3) % 4}, {"gy": (gy + 1) % 4}
+    pl.when(has_m)(lambda: greet(to_m))
+    pl.when(has_p)(lambda: greet(to_p))
     for target in greeted:
-        pl.semaphore_signal(barrier, inc=1, device_id=target, device_id_type=MESH)
+        greet(target)
 
     loads = [
         pltpu.make_async_copy(src, dst, load_sem.at[i])
         for i, (src, dst) in enumerate((
             (density, r0), (labels_hbm, labels), (value_hbm, val), (turn_hbm, turn), (ax_hbm, axt), (ay_hbm, ayt),
             (coupling_hbm, coupling), (kernel_hbm, kern),
+            (counts_hbm, counts),
         ))
     ]
     for c in loads:
@@ -98,10 +118,6 @@
             src_ref=src, dst_ref=dst, send_sem=ss.at[i], recv_sem=rs.at[i], device_id=target, device_id_type=MESH
         )
 
-    has_m, has_p = gx > 0, gx < 7
-    west, east = gy > 0, gy < 3
-    to_m, to_p = {"gx": (gx + 7) % 8}, {"gx": (gx + 1) % 8}
-    to_w, to_e = {"gy": (gy + 3) % 4}, {"gy": (gy + 1) % 4}
     lane = lax.broadcasted_iota(I32, (X, Y), 1)
     row = lax.broadcasted_iota(I32, (X, Y), 0)
     lane_h = lax.broadcasted_iota(I32, (32, Y), 1)
@@ -140,7 +156,7 @@
     for k0, dst, shift in ((0, sy_p, 65), (2, sy_m, 64)):
         def pack(j, acc, k0=k0):
             return pack_column(acc, r0[k0 * 16 + j], j, k0)
-        acc = lax.fori_loop(0, 32, pack, zero_plane, unroll=4)
+        acc = lax.fori_loop(0, 32, pack, zero_plane, unroll=32)
         dst[0:32, :] = jnp.where(lane == 64, pltpu.roll(opened, shift, 1), acc)
 
     def value_row(i):
@@ -212,30 +228,38 @@
         (copy(VAL_UP, sv_m, hv_p, to_m), jnp.logical_and(low, has_m), jnp.logical_and(high, has_p)),
     )
 
-    def start(c, condition):
-        @pl.when(condition)
-        def _():
-            c.start()
-
-    def wait_recv(c, condition):
-        @pl.when(condition)
-        def _():
-            c.wait_recv()
-
-    def wait_send(c, condition):
-        @pl.when(condition)
-        def _():
-            c.wait_send()
-
-    pl.semaphore_wait(barrier, len(greeted))
-    for c, sends, _ in first:
-        start(c, sends)
+    started, landed = [], set()
+
+    def guarded(condition, act):
+        if condition is True:
+            act()
+        else:
+            pl.when(condition)(act)
+
+    def launch(c, sends=True, receives=True):
+        guarded(sends, c.start)
+        started.append((c, sends, receives))
+        return len(started) - 1
+
+    def land(n):
+        c, _, receives = started[n]
+        guarded(receives, c.wait_recv)
+        landed.add(n)
+
+    def finish_all():
+        for n, (c, sends, _) in enumerate(started):
+            if n not in landed:
+                land(n)
+            guarded(sends, c.wait_send)
+
+    pl.semaphore_wait(barrier, len(greeted) + has_m.astype(I32) + has_p.astype(I32))
+    first = [launch(*c) for c in first]
     for c in loads[3:]:
         c.wait()
     kf[:, 0:64] = kern[...]
     kf[:, 64:128] = kern[...]
-    for c, _, receives in first[:4]:
-        wait_recv(c, receives)
+    for n in first[:4]:
+        land(n)
 
     open_p = jnp.where(row == X - 1, hx_p[32:33, :], pltpu.roll(opened, X - 1, 0))
     open_m = jnp.where(row == 0, hx_m[32:33, :], pltpu.roll(opened, 1, 0))
@@ -287,7 +311,7 @@
             acc = finish(j - 1, partial, down, acc)
             return s + up_last, up, acc
 
-        partial, _, acc = lax.fori_loop(1, 16, body, carry, unroll=3)
+        partial, _, acc = lax.fori_loop(1, 16, body, carry, unroll=15)
         _, _, down = turns((h0 + 16) % 64)
         return finish(15, partial, down, acc)
 
@@ -306,28 +330,21 @@
             columns = (copy(STEP_COL + k, s2y.at[k], h2y.at[k], to_e), east, west)
         else:
             columns = (copy(STEP_COL + k, s2y.at[k], h2y.at[k], to_w), west, east)
-        for c, sends, receives in (rows, columns):
-            start(c, sends)
-            second.append((c, sends, receives))
-
-    over_y = [[], [], [], []]
-    stores = []
+        second += [launch(*rows), launch(*columns)]
+
+    over_y = [[] for _ in range(CHUNKS)]
     for k in range(4):
-        for c, _, receives in second[2 * k:2 * k + 2]:
-            wait_recv(c, receives)
+        for n in second[2 * k:2 * k + 2]:
+            land(n)
         transport(k, r1, r2, h2x, None, h2y, None, False)
-        block = pl.ds(16 * k, 16)
-        c = pltpu.make_async_copy(r2.at[block], moved.at[block], out_sem.at[k])
-        c.start()
-        stores.append(c)
-        for d in (2, 1, 3):
-            yy = (y + d) % 4
-            qq = jnp.where(odd == 1, 3 - yy, yy)
-            part = r2[block, pl.ds(pl.multiple_of(qq * 8, 8), 8), :]
-            ysend[k, d - 1] = encode(part.reshape(128, Y) * (1.0 / BOUND))
-            c = copy(OVER_Y + 3 * k + d - 1, ysend.at[k, d - 1], yrecv.at[k, d - 1], at(zh, yy))
-            c.start()
-            over_y[k].append(c)
+        for c in range(k * CHUNKS // 4, (k + 1) * CHUNKS // 4):
+            for d in (2, 1, 3):
+                yy = (y + d) % 4
+                qq = jnp.where(odd == 1, 3 - yy, yy)
+                part = r2[pl.ds(CHUNK * c, CHUNK), pl.ds(pl.multiple_of(qq * 8, 8), 8), :]
+                ysend[c, d - 1] = encode(part.reshape(ROWS, Y) * (1.0 / BOUND))
+                there = copy(OVER_Y + 3 * c + d - 1, ysend.at[c, d - 1], yrecv.at[c, d - 1], at(zh, yy))
+                over_y[c].append(launch(there))
 
     def count(z, yy):
         return counts[z * 4 + yy].astype(F32)
@@ -344,22 +361,20 @@
     inverse_mine = (1.0 / BOUND) / plane_of(mine)
 
     def scaled(part, factor):
-        return (part.reshape(16, 8, Y) * factor).reshape(128, Y)
-
-    over_z = [[None, None] for _ in range(4)]
-    for k in range(4):
-        block = pl.ds(16 * k, 16)
-        part = r2[block, pl.ds(pl.multiple_of(q * 8, 8), 8), :].reshape(128, Y) * count(zh, y)
-        for c, d in zip(over_y[k], (2, 1, 3)):
-            c.wait_recv()
-            part = part + decode(yrecv[k, d - 1]) * count(zh, (y + 4 - d) % 4)
-        zsend[k, 0] = encode(scaled(part, inverse_mine))
-        c = copy(OVER_Z + 2 * k, zsend.at[k, 0], zrecv.at[k, 0], at(pair[k % 2], y))
-        c.start()
-        over_z[k][0] = c
-
-    wait_recv(first[4][0], first[4][2])
-    wait_recv(first[5][0], first[5][2])
+        return (part.reshape(CHUNK, 8, Y) * factor).reshape(ROWS, Y)
+
+    over_z = [[None, None] for _ in range(CHUNKS)]
+    for c in range(CHUNKS):
+        block = pl.ds(CHUNK * c, CHUNK)
+        part = r2[block, pl.ds(pl.multiple_of(q * 8, 8), 8), :].reshape(ROWS, Y) * count(zh, y)
+        for n, d in zip(over_y[c], (2, 1, 3)):
+            land(n)
+            part = part + decode(yrecv[c, d - 1]) * count(zh, (y + 4 - d) % 4)
+        zsend[c, 0] = encode(scaled(part, inverse_mine))
+        over_z[c][0] = launch(copy(OVER_Z + 2 * c, zsend.at[c, 0], zrecv.at[c, 0], at(pair[c % 2], y)))
+
+    land(first[4])
+    land(first[5])
 
     @pl.when(low)
     def _():
@@ -425,27 +440,25 @@
 
     lower = [jnp.full((8, Y), zh, I32) < jnp.full((8, Y), p, I32) for p in pair]
 
-    def merge(k, stage, partner, weight_own, weight_other):
-        a = decode(zsend[k, stage]).reshape(16, 8, Y) * weight_own
-        b = decode(zrecv[k, stage]).reshape(16, 8, Y) * weight_other
+    def merge(c, stage, partner, weight_own, weight_other):
+        a = decode(zsend[c, stage]).reshape(CHUNK, 8, Y) * weight_own
+        b = decode(zrecv[c, stage]).reshape(CHUNK, 8, Y) * weight_other
         is_low = lower[partner]
         return jnp.where(is_low, a, b) + jnp.where(is_low, b, a)
 
-    for k in range(4):
-        p = k % 2
-        over_z[k][0].wait_recv()
-        both = merge(k, 0, p, mine, across[p])
-        factor = (1.0 / BOUND) / plane_of(mine + across[p])
-        zsend[k, 1] = encode((both * factor).reshape(128, Y))
-        c = copy(OVER_Z + 2 * k + 1, zsend.at[k, 1], zrecv.at[k, 1], at(pair[1 - p], y))
-        c.start()
-        over_z[k][1] = c
-    for k in range(4):
-        p = k % 2
-        over_z[k][1].wait_recv()
+    factors = [(1.0 / BOUND) / plane_of(mine + across[p]) for p in range(2)]
+    for c in range(CHUNKS):
+        p = c % 2
+        land(over_z[c][0])
+        both = merge(c, 0, p, mine, across[p])
+        zsend[c, 1] = encode((both * factors[p]).reshape(ROWS, Y))
+        over_z[c][1] = launch(copy(OVER_Z + 2 * c + 1, zsend.at[c, 1], zrecv.at[c, 1], at(pair[1 - p], y)))
+    for c in range(CHUNKS):
+        p = c % 2
+        land(over_z[c][1])
         here = mine + across[p]
-        mixed = merge(k, 1, 1 - p, here, everyone - here) * inverse_all
-        total[pl.ds(128 * k, 128), :] = mixed.reshape(128, Y)
+        mixed = merge(c, 1, 1 - p, here, everyone - here) * inverse_all
+        total[pl.ds(ROWS * c, ROWS), :] = mixed.reshape(ROWS, Y)
 
     mixed_rows = jnp.concatenate([total[pl.ds(i, H, stride=8), :] for i in range(8)], axis=1)
     running = 0.5 + 0.5 * jnp.dot(kb, widen(mixed_rows), preferred_element_type=F32)
@@ -463,89 +476,99 @@
         (copy(REPLY + 2, sc_p, hc_m, to_e), east, west),
         (copy(REPLY + 3, sc_m, hc_p, to_w), west, east),
     )
-    for c, sends, _ in edges:
-        start(c, sends)
-    for c, _, receives in edges:
-        wait_recv(c, receives)
+    edges = [launch(*c) for c in edges]
+    for n in edges:
+        land(n)
 
     out_rows = out.reshape(H * X, Y)
 
-    def unpack(codes, qq, half):
-        scale = codes[256:257, :].astype(F32) * (0.125 / 32767.0)
-        for n in range(4):
-            v = codes[64 * n:64 * n + 64, :].astype(F32) * scale
-            out_rows[pl.ds(qq * 8 + 4 * half + n, H, stride=X), :] = v
+    def unpack(codes, qq, piece):
+        scale = codes[MARK:MARK + 1, :].astype(F32) * (0.125 / 32767.0)
+        for n in range(SPAN):
+            v = codes[H * n:H * n + H, :].astype(F32) * scale
+            out_rows[pl.ds(qq * 8 + SPAN * piece + n, H, stride=X), :] = v
 
     gathers = []
-    for half in range(2):
-        indices = range(4 * half, 4 * half + 4)
+    for piece in range(PIECES):
+        indices = range(SPAN * piece, SPAN * piece + SPAN)
         twice = reply(once, hr_m[...], hr_p[...], hc_m[...], hc_p[...], indices)
         twice = [(cost[i] + t) * keep_rows[i:i + 1, :] for i, t in zip(indices, twice)]
         top = jnp.max(jnp.abs(jnp.concatenate(twice, axis=0)), axis=0, keepdims=True)
         eighths = (top * 8.0).astype(I32) + 1
         inverse = (32767.0 * 8.0) / eighths.astype(F32)
-        for n in range(4):
+        for n in range(SPAN):
             code = (twice[n] * inverse + 32768.5).astype(I32) - 32768
-            gsend[half, pl.ds(64 * n, 64), :] = code.astype(I16)
-        gsend[half, pl.ds(256, 16), :] = jnp.broadcast_to(eighths, (16, Y)).astype(I16)
+            gsend[piece, pl.ds(H * n, H), :] = code.astype(I16)
+        gsend[piece, pl.ds(MARK, 16), :] = jnp.broadcast_to(eighths, (16, Y)).astype(I16)
         for d in (2, 1, 3):
-            c = copy(GATHER + 3 * half + d - 1, gsend.at[half], grecv.at[half, d - 1], at(zh, (y + d) % 4))
-            c.start()
-            gathers.append((c, half, d))
-    for half in range(2):
-        unpack(gsend[half].astype(I32), q, half)
-    for c, half, d in gathers:
-        c.wait_recv()
+            there = copy(GATHER + 3 * piece + d - 1, gsend.at[piece], grecv.at[piece, d - 1], at(zh, (y + d) % 4))
+            gathers.append((launch(there), piece, d))
+    for piece in range(PIECES):
+        unpack(gsend[piece].astype(I32), q, piece)
+    for n, piece, d in gathers:
+        land(n)
         yy = (y + 4 - d) % 4
-        unpack(grecv[half, d - 1].astype(I32), jnp.where(odd == 1, 3 - yy, yy), half)
-    c = pltpu.make_async_copy(out, values, out_sem.at[4])
-    c.start()
-    stores.append(c)
-
-    for c, sends, _ in (*first, *second, *edges):
-        wait_send(c, sends)
-    for k in range(4):
-        for c in (*over_y[k], *over_z[k]):
-            c.wait_send()
-    for c, _, _ in gathers:
-        c.wait_send()
-    for c in stores:
+        unpack(grecv[piece, d - 1].astype(I32), jnp.where(odd == 1, 3 - yy, yy), piece)
+    finish_all()
+
+
+def write_out(moved, values, moved_out, values_out, sems):
+    copies = [
+        pltpu.make_async_copy(src, dst, sems.at[i])
+        for i, (src, dst) in enumerate(((moved, moved_out), (values, values_out)))
+    ]
+    for c in copies:
+        c.start()
+    for c in copies:
         c.wait()
 
 
 def shards(density, turn_rate, value_init, labels, counts, kernel_matrix):
     along_x, along_y, coupling = tables()
     vmem = lambda *shape: pltpu.VMEM(shape, F32)
-    anywhere = pl.BlockSpec(memory_space=pl.ANY)
+    in_hbm = pl.BlockSpec(memory_space=pltpu.HBM)
     scratch = [
         vmem(H, X, Y), pltpu.VMEM((H, X, Y), BF16), vmem(H, X, Y), pltpu.VMEM((X, Y), I32), vmem(H, Y), vmem(H, Y),
         vmem(H, H), vmem(H, H),
         vmem(40, Y), vmem(40, Y), vmem(64, Y), vmem(64, Y), vmem(32, Y), vmem(32, Y),
         vmem(40, Y), vmem(40, Y), vmem(64, Y), vmem(64, Y), vmem(32, Y), vmem(32, Y),
-        vmem(H, X, Y), vmem(H, X, Y), vmem(4, 16, Y), vmem(4, X, Y), vmem(4, 16, Y), vmem(4, X, Y), vmem(4, X, Y),
+        vmem(H, X, Y), vmem(4, 16, Y), vmem(4, X, Y), vmem(4, 16, Y), vmem(4, X, Y), vmem(4, X, Y),
         vmem(X, Y),
-        pltpu.VMEM((4, 3, 128, Y), I16), pltpu.VMEM((4, 3, 128, Y), I16),
-        pltpu.VMEM((4, 2, 128, Y), I16), pltpu.VMEM((4, 2, 128, Y), I16), vmem(512, Y), vmem(8, H, Y),
+        pltpu.VMEM((CHUNKS, 3, ROWS, Y), I16), pltpu.VMEM((CHUNKS, 3, ROWS, Y), I16),
+        pltpu.VMEM((CHUNKS, 2, ROWS, Y), I16), pltpu.VMEM((CHUNKS, 2, ROWS, Y), I16), vmem(512, Y), vmem(8, H, Y),
         vmem(32, Y), vmem(32, Y), vmem(8, Y), vmem(H, 128), vmem(H, 128),
         *[vmem(32, Y) for _ in range(8)],
-        pltpu.VMEM((2, 272, Y), I16), pltpu.VMEM((2, 3, 272, Y), I16), vmem(H, X, Y),
-        pltpu.SemaphoreType.DMA((8,)), pltpu.SemaphoreType.DMA((5,)),
+        pltpu.VMEM((PIECES, MARK + 16, Y), I16), pltpu.VMEM((PIECES, 3, MARK + 16, Y), I16),
+        pltpu.SMEM((16,), I32), pltpu.SemaphoreType.DMA((9,)),
         pltpu.SemaphoreType.DMA((COPIES,)), pltpu.SemaphoreType.DMA((COPIES,)),
     ]
+    held = pltpu.VMEM((H, X, Y), F32)
+    in_vmem = pl.BlockSpec(memory_space=pltpu.VMEM)
+    operands = (
+        counts, density[0], turn_rate[0], value_init, labels,
+        jnp.asarray(along_x), jnp.asarray(along_y), jnp.asarray(coupling), kernel_matrix,
+    )
     moved, values = pl.pallas_call(
         kernel,
-        out_shape=(jax.ShapeDtypeStruct((H, X, Y), F32), jax.ShapeDtypeStruct((H, X, Y), F32)),
-        in_specs=[pl.BlockSpec(memory_space=pltpu.SMEM)] + [anywhere] * 8,
-        out_specs=(anywhere, anywhere),
+        out_shape=(held, held),
+        in_specs=[in_hbm] * 9,
+        out_specs=(in_vmem, in_vmem),
         scratch_shapes=scratch,
         compiler_params=pltpu.CompilerParams(
             collective_id=1, has_side_effects=True, vmem_limit_bytes=40 * 1024 * 1024
         ),
         name="play",
-    )(
-        counts, density[0], turn_rate[0], value_init, labels,
-        jnp.asarray(along_x), jnp.asarray(along_y), jnp.asarray(coupling), kernel_matrix,
-    )
+    )(*[pltpu.with_memory_space_constraint(a, pltpu.HBM) for a in operands])
+    whole = jax.ShapeDtypeStruct((H, X, Y), F32)
+    moved, values = pl.pallas_call(
+        write_out,
+        out_shape=(whole, whole),
+        in_specs=[in_vmem, in_vmem],
+        out_specs=(in_hbm, in_hbm),
+        scratch_shapes=[pltpu.SemaphoreType.DMA((2,))],
+        compiler_params=pltpu.CompilerParams(vmem_limit_bytes=8 * 1024 * 1024),
+        name="write",
+    )(moved, values)
     return moved[None], values
 
 

time: 66.3 us -> 54.4 us (0.82)
  local copies, waits for them, and re-layouts: 9.83 us -> 0 us
  Pallas kernels: 55.2 us -> 53.6 us
    unnamed x20 -> x0, local copies, waits for them, and re-layouts: 9.83 us -> none
    pallas_call x1 -> x2, Pallas kernels: 55.2 us -> 53.6 us  [the longest x1 52.2 us: shards(): pl.pallas_call(kernel, out_shape=(held, held), in_specs=[in_hbm] * 9, out...]
where the time goes in v2:
time: 54.4 us; the launch traced here: 54.2 us
  Pallas kernels  53.6 us (99%)
  between operations  0.64 us (1%)
    pallas_call x1, Pallas kernels, shards(): pl.pallas_call(kernel, out_shape=(held, held), in_specs=[in_hbm] * 9, out...  52.2 us
    pallas_call x1, Pallas kernels, shards(): pl.pallas_call(write_out, out_shape=(whole, whole), in_specs=[in_vmem, in...  1.33 us

profile of v2, /device:TPU:10, one launch (start us, length us, event | category | flops | bytes accessed | tf_op | source)
XLA Modules:
  0.0 54.2 jit_solution(16501461300438181186)
XLA Ops:
  0.6 52.2 %play.1 = (f32[64,32,128]{2,1,0:T(8,128)S(1)}, f32[64,32,128]{2,1,0:T(8,128)S(1)}) custom-call(s32[16]{0:T(128)} %counts_hbm.1, f32[64,32,128]{2,1,0:T(8,128)} %bitcast.3, bf16[64,32,128]{2,1,0:T(8,128)(2,1)} %bitcast.4, f32[64,32,128]{2,1,0:T(8,128)} %value_hbm.1, s32[32,128]{1,0:T(8,128)} %labels_hbm.1, f32[64,128]{1,0:T(8,128)} %constant.6.clone.ax_hbm, ...), custom_call_target="tpu_custom_call" | custom-call | tf_op jit(solution)/shard_map/play/pallas_call | solution.py:551
  52.9 1.3 %write.1 = (f32[64,32,128]{2,1,0:T(8,128)}, f32[64,32,128]{2,1,0:T(8,128)}) custom-call(f32[64,32,128]{2,1,0:T(8,128)S(1)} %get-tuple-element.6.moved, f32[64,32,128]{2,1,0:T(8,128)S(1)} %get-tuple-element.7.values), custom_call_target="tpu_custom_call" | custom-call | tf_op jit(solution)/shard_map/write/pallas_call | solution.py:563

commit v3 on v2

--- a/solution.py
+++ b/solution.py
@@ -16,11 +16,11 @@
 SPEED = 0.55
 BOUND = 9.5
 
-ROW_UP, ROW_DOWN, COL_UP, COL_DOWN, VAL_UP, VAL_DOWN = range(6)
+ROW_UP, ROW_DOWN, COL_UP, COL_DOWN, VAL_UP, VAL_DOWN, VALCOL_UP, VALCOL_DOWN = range(8)
 CHUNK = 8
 CHUNKS = H // CHUNK
 ROWS = 8 * CHUNK
-STEP_ROW, STEP_COL, OVER_Y = 6, 10, 14
+STEP_ROW, STEP_COL, OVER_Y = 8, 12, 16
 OVER_Z = OVER_Y + 3 * CHUNKS
 REPLY = OVER_Z + 2 * CHUNKS
 GATHER = REPLY + 4
@@ -65,7 +65,7 @@
     counts_hbm, density, turn_hbm, value_hbm, labels_hbm, ax_hbm, ay_hbm, coupling_hbm, kernel_hbm,
     r2, out,
     r0, turn, val, labels, axt, ayt, coupling, kern,
-    sx_m, sx_p, sy_m, sy_p, sv_m, sv_p, hx_m, hx_p, hy_m, hy_p, hv_m, hv_p,
+    sx_m, sx_p, sy_m, sy_p, sv_m, sv_p, svc_m, svc_p, hx_m, hx_p, hy_m, hy_p, hv_m, hv_p, hvc_m, hvc_p,
     r1, s2x, s2y, h2x, h2y, weights, keep,
     ysend, yrecv, zsend, zrecv, total, base,
     up_row, down_row, cs, kf, cf,
@@ -157,7 +157,7 @@
         def pack(j, acc, k0=k0):
             return pack_column(acc, r0[k0 * 16 + j], j, k0)
         acc = lax.fori_loop(0, 32, pack, zero_plane, unroll=32)
-        dst[0:32, :] = jnp.where(lane == 64, pltpu.roll(opened, shift, 1), acc)
+        dst[...] = jnp.where(lane == 64, pltpu.roll(opened, shift, 1), acc)
 
     def value_row(i):
         return val.reshape(H * X, Y)[pl.ds(q * 8 + i, H, stride=X), :]
@@ -170,54 +170,10 @@
             acc = jnp.where(lane_h == i, pltpu.roll(part, shift, 1) if shift else part, acc)
         return acc
 
-    loads[2].wait()
-    own = [value_row(i) for i in range(8)]
-    sy_p[32:64, :] = pack_values(own, 32, True)
-    sy_m[32:64, :] = pack_values(own, 0, False)
-    sv_p[...] = own[7][16:48, :]
-    sv_m[0:16, :] = own[0][0:16, :]
-    sv_m[16:32, :] = own[0][48:64, :]
-
-    @pl.when(gx == 0)
-    def _():
-        hx_m[...] = jnp.zeros((40, Y), F32)
-        hv_m[...] = jnp.zeros((32, Y), F32)
-        h2x[0] = jnp.zeros((16, Y), F32)
-        h2x[3] = jnp.zeros((16, Y), F32)
-
-    @pl.when(gx == 7)
-    def _():
-        hx_p[...] = jnp.zeros((40, Y), F32)
-        hv_p[...] = jnp.zeros((32, Y), F32)
-        h2x[1] = jnp.zeros((16, Y), F32)
-        h2x[2] = jnp.zeros((16, Y), F32)
-
-    @pl.when(gy == 0)
-    def _():
-        hy_m[...] = jnp.zeros((64, Y), F32)
-        hc_m[...] = jnp.zeros((32, Y), F32)
-        h2y[0] = zero_plane
-        h2y[1] = zero_plane
-
-    @pl.when(gy == 3)
-    def _():
-        hy_p[...] = jnp.zeros((64, Y), F32)
-        hc_p[...] = jnp.zeros((32, Y), F32)
-        h2y[2] = zero_plane
-        h2y[3] = zero_plane
-
     low, high = q == 0, q == 3
     near_up = {"member": zh * 4 + jnp.where(low, y, (y + 4 - turn_sign) % 4), "gx": jnp.where(low, (gx + 7) % 8, gx)}
     near_down = {"member": zh * 4 + jnp.where(high, y, (y + turn_sign) % 4), "gx": jnp.where(high, (gx + 1) % 8, gx)}
     has_up, has_down = jnp.logical_or(q > 0, has_m), jnp.logical_or(q < 3, has_p)
-
-    @pl.when(jnp.logical_not(has_up))
-    def _():
-        hr_m[...] = jnp.zeros((32, Y), F32)
-
-    @pl.when(jnp.logical_not(has_down))
-    def _():
-        hr_p[...] = jnp.zeros((32, Y), F32)
 
     first = (
         (copy(ROW_DOWN, sx_p, hx_m, to_p), has_p, has_m),
@@ -226,6 +182,8 @@
         (copy(COL_UP, sy_m, hy_p, to_w), west, east),
         (copy(VAL_DOWN, sv_p, hv_m, to_p), jnp.logical_and(high, has_p), jnp.logical_and(low, has_m)),
         (copy(VAL_UP, sv_m, hv_p, to_m), jnp.logical_and(low, has_m), jnp.logical_and(high, has_p)),
+        (copy(VALCOL_DOWN, svc_p, hvc_m, to_e), east, west),
+        (copy(VALCOL_UP, svc_m, hvc_p, to_w), west, east),
     )
 
     started, landed = [], set()
@@ -253,31 +211,70 @@
             guarded(sends, c.wait_send)
 
     pl.semaphore_wait(barrier, len(greeted) + has_m.astype(I32) + has_p.astype(I32))
-    first = [launch(*c) for c in first]
+    begun = [launch(*c) for c in first[:4]]
+    @pl.when(gx == 0)
+    def _():
+        hx_m[...] = jnp.zeros((40, Y), F32)
+        hv_m[...] = jnp.zeros((32, Y), F32)
+        for k in (0, 3):
+            h2x[k] = jnp.zeros((16, Y), F32)
+
+    @pl.when(gx == 7)
+    def _():
+        hx_p[...] = jnp.zeros((40, Y), F32)
+        hv_p[...] = jnp.zeros((32, Y), F32)
+        for k in (1, 2):
+            h2x[k] = jnp.zeros((16, Y), F32)
+
+    @pl.when(gy == 0)
+    def _():
+        for ref in (hy_m, h2y.at[0], h2y.at[1], hvc_m, hc_m):
+            ref[...] = zero_plane
+
+    @pl.when(gy == 3)
+    def _():
+        for ref in (hy_p, h2y.at[2], h2y.at[3], hvc_p, hc_p):
+            ref[...] = zero_plane
+
+    @pl.when(jnp.logical_not(has_up))
+    def _():
+        hr_m[...] = jnp.zeros((32, Y), F32)
+
+    @pl.when(jnp.logical_not(has_down))
+    def _():
+        hr_p[...] = jnp.zeros((32, Y), F32)
+
+    loads[2].wait()
+    own = [value_row(i) for i in range(8)]
+    svc_p[...] = pack_values(own, 32, True)
+    svc_m[...] = pack_values(own, 0, False)
+    sv_p[...] = own[7][16:48, :]
+    sv_m[0:16, :] = own[0][0:16, :]
+    sv_m[16:32, :] = own[0][48:64, :]
+    begun += [launch(*c) for c in first[4:]]
     for c in loads[3:]:
         c.wait()
     kf[:, 0:64] = kern[...]
     kf[:, 64:128] = kern[...]
-    for n in first[:4]:
+    for n in begun[:4]:
         land(n)
 
     open_p = jnp.where(row == X - 1, hx_p[32:33, :], pltpu.roll(opened, X - 1, 0))
     open_m = jnp.where(row == 0, hx_m[32:33, :], pltpu.roll(opened, 1, 0))
-    open_e = jnp.where(lane == Y - 1, pltpu.roll(hy_p[0:32, :], 63, 1), pltpu.roll(opened, Y - 1, 1))
-    open_w = jnp.where(lane == 0, pltpu.roll(hy_m[0:32, :], 64, 1), pltpu.roll(opened, 1, 1))
+    open_e = jnp.where(lane == Y - 1, pltpu.roll(hy_p[...], 63, 1), pltpu.roll(opened, Y - 1, 1))
+    open_w = jnp.where(lane == 0, pltpu.roll(hy_m[...], 64, 1), pltpu.roll(opened, 1, 1))
     weights[0] = opened * open_p
     weights[1] = opened * open_m
     weights[2] = opened * open_e
     weights[3] = opened * open_w
 
-    def transport(k, src, dst, halo_x, x_at, halo_y, y_at, pack):
+    def transport(k, src, dst, halo_x, x_at, halo_y, y_at, packed):
         out_x, in_x = (0, 1) if k in (0, 3) else (1, 0)
         out_y, in_y = (2, 3) if k in (0, 1) else (3, 2)
         wox, wix, woy, wiy = weights[out_x], weights[in_x], weights[out_y], weights[in_y]
         kept = keep[...]
-        columns = halo_y[0:32, :] if y_at is not None else halo_y[k]
+        columns = halo_y[...]
         h0 = 16 * k
-        y_from = 0 if y_at is None else y_at
 
         def turns(h):
             r = src[h]
@@ -290,20 +287,20 @@
             r, up, down = turns(h)
             ax = axt[pl.ds(h, 1), :]
             ay = ayt[pl.ds(h, 1), :]
-            hx = halo_x[pl.ds(x_at + j, 1), :] if x_at is not None else halo_x[k, pl.ds(j, 1), :]
+            hx = halo_x[pl.ds(x_at + j, 1), :]
             xn = shift_x(r, hx, k)
-            yn = shift_y(r, columns, y_from + j, k)
+            yn = shift_y(r, columns, y_at + j, k)
             s = r - up - down + ax * (wix * xn - wox * r) + ay * (wiy * yn - woy * r)
             return s, up, down
 
         _, up_before, _ = turns((h0 + 63) % 64)
         s, up, _ = start_of(0)
-        carry = (s + up_before, up, zero_plane)
+        carry = (s + up_before, up, zero_plane if packed is None else packed)
 
         def finish(j, partial, down, acc):
             new = (partial + down) * kept
             dst[h0 + j] = new
-            return pack_column(acc, new, j, k) if pack else acc
+            return acc if packed is None else pack_column(acc, new, y_at + j, k)
 
         def body(j, carry):
             partial, up_last, acc = carry
@@ -315,28 +312,26 @@
         _, _, down = turns((h0 + 16) % 64)
         return finish(15, partial, down, acc)
 
+    def halos(k, row_m, row_p, column_m, column_p):
+        return (
+            ((row_m, 0), (row_p, 0), (row_p, 16), (row_m, 16))[k]
+            + ((column_m, 0), (column_m, 16), (column_p, 0), (column_p, 16))[k]
+        )
+
     second = []
     for k in range(4):
-        halo_x, x_at = ((hx_m, 0), (hx_p, 0), (hx_p, 16), (hx_m, 16))[k]
-        halo_y, y_at = ((hy_m, 0), (hy_m, 16), (hy_p, 0), (hy_p, 16))[k]
-        acc = transport(k, r0, r1, halo_x, x_at, halo_y, y_at, True)
-        s2y[k] = acc
+        s2y[k] = transport(k, r0, r1, *halos(k, hx_m, hx_p, hy_m, hy_p), zero_plane)
         s2x[k] = rows_of(r1, 16 * k, 16, X - 1 if k in (0, 3) else 0)
-        if k in (0, 3):
-            rows = (copy(STEP_ROW + k, s2x.at[k], h2x.at[k], to_p), has_p, has_m)
-        else:
-            rows = (copy(STEP_ROW + k, s2x.at[k], h2x.at[k], to_m), has_m, has_p)
-        if k in (0, 1):
-            columns = (copy(STEP_COL + k, s2y.at[k], h2y.at[k], to_e), east, west)
-        else:
-            columns = (copy(STEP_COL + k, s2y.at[k], h2y.at[k], to_w), west, east)
-        second += [launch(*rows), launch(*columns)]
+        target = (to_p, has_p, has_m) if k in (0, 3) else (to_m, has_m, has_p)
+        second.append(launch(copy(STEP_ROW + k, s2x.at[k], h2x.at[k], target[0]), *target[1:]))
+        target = (to_e, east, west) if k in (0, 1) else (to_w, west, east)
+        second.append(launch(copy(STEP_COL + k, s2y.at[k], h2y.at[k], target[0]), *target[1:]))
 
     over_y = [[] for _ in range(CHUNKS)]
     for k in range(4):
         for n in second[2 * k:2 * k + 2]:
             land(n)
-        transport(k, r1, r2, h2x, None, h2y, None, False)
+        transport(k, r1, r2, h2x.at[k], 0, h2y.at[k], (0, 16, 0, 16)[k], None)
         for c in range(k * CHUNKS // 4, (k + 1) * CHUNKS // 4):
             for d in (2, 1, 3):
                 yy = (y + d) % 4
@@ -373,8 +368,8 @@
         zsend[c, 0] = encode(scaled(part, inverse_mine))
         over_z[c][0] = launch(copy(OVER_Z + 2 * c, zsend.at[c, 0], zrecv.at[c, 0], at(pair[c % 2], y)))
 
-    land(first[4])
-    land(first[5])
+    for n in begun[4:]:
+        land(n)
 
     @pl.when(low)
     def _():
@@ -404,37 +399,63 @@
     cf_high, cf_low = split_left(cf[...])
     cb = jnp.concatenate([cf_high, cf_low], axis=1)
 
-    def reply(rows, before, after, first_column, last_column, indices):
-        lowest_of, columns = [], []
-        for i in indices:
-            v = rows[i]
-            prior = rows[i - 1][16:48, :] if i > 0 else before
-            if i < 7:
-                later = (rows[i + 1][0:16, :], rows[i + 1][48:64, :])
-            else:
-                later = (after[0:16, :], after[16:32, :])
-            lane_of = lax.broadcasted_iota(I32, (32, Y), 1)
-            north = jnp.where(lane_of == Y - 1, pltpu.roll(last_column, Y - 1 - i, 1), pltpu.roll(v[0:32, :], Y - 1, 1))
-            west_column = pltpu.roll(first_column, Y - i, 1) if i else first_column
-            south = jnp.where(lane_of == 0, west_column, pltpu.roll(v[32:64, :], 1, 1))
+    lane_of = lax.broadcasted_iota(I32, (32, Y), 1)
+
+    def around(rows, before, after, first_column, last_column, i):
+        v = rows[i]
+        prior = rows[i - 1][16:48, :] if i > 0 else before
+        if i < 7:
+            later = (rows[i + 1][0:16, :], rows[i + 1][48:64, :])
+        else:
+            later = (after[0:16, :], after[16:32, :])
+        north, south = pltpu.roll(v[0:32, :], Y - 1, 1), pltpu.roll(v[32:64, :], 1, 1)
+        if last_column is not None:
+            north = jnp.where(lane_of == Y - 1, pltpu.roll(last_column, Y - 1 - i, 1), north)
+            south = jnp.where(lane_of == 0, pltpu.roll(first_column, Y - i, 1) if i else first_column, south)
+        return v, prior, later, north, south, [w[i:i + 1, :] for w in w_rows]
+
+    def reply(jobs):
+        lowest_of, parts = [], []
+        for v, prior, later, north, south, w in jobs:
             moves = []
             for k in range(4):
                 part = slice(16 * k, 16 * k + 16)
                 vk = v[part, :]
                 xn = (later[0], prior[0:16, :], prior[16:32, :], later[1])[k]
                 yn = (north[0:16, :], north[16:32, :], south[0:16, :], south[16:32, :])[k]
-                wx = w_rows[0 if k in (0, 3) else 1][i:i + 1, :]
-                wy = w_rows[2 if k in (0, 1) else 3][i:i + 1, :]
+                wx = w[0 if k in (0, 3) else 1]
+                wy = w[2 if k in (0, 1) else 3]
                 moves.append(vk + axt[part, :] * (wx * (xn - vk)) + ayt[part, :] * (wy * (yn - vk)))
             moves = jnp.concatenate(moves, axis=0)
             lowest = jnp.min(moves, axis=0, keepdims=True)
             lowest_of.append(lowest)
-            columns.append(jnp.exp((lowest - moves) * 10.0))
-        summed = jnp.dot(cb, widen(jnp.concatenate(columns, axis=1)), preferred_element_type=F32)
+            parts.append(jnp.exp((lowest - moves) * 10.0))
+        summed = jnp.dot(cb, widen(jnp.concatenate(parts, axis=1)), preferred_element_type=F32)
         logs = jnp.log(summed) * 0.1
-        return [lowest_of[n] - logs[:, n * Y:(n + 1) * Y] for n in range(len(indices))]
-
-    from_start = reply(own, up_row[...], down_row[...], hy_m[32:64, :], hy_p[32:64, :], range(8))
+        return [lowest_of[n] - logs[:, n * Y:(n + 1) * Y] for n in range(len(jobs))]
+
+    row_8 = lax.broadcasted_iota(I32, (8, Y), 0)
+    lane_8 = lax.broadcasted_iota(I32, (8, Y), 1)
+
+    def sides_of(w):
+        first = jnp.where(lane_8 == row_8, w[:, 0:1], 0.0)
+        last = jnp.where(lane_8 == row_8 + 8, w[:, Y - 1:Y], 0.0)
+        return jnp.sum(first + last, axis=0, keepdims=True)
+
+    w_sides = [sides_of(w) for w in w_rows]
+    keep_sides = sides_of(keep_rows)
+
+    def side_by_side(rows, first, last, part):
+        acc = jnp.zeros((part.stop - part.start, Y), F32)
+        lanes = lax.broadcasted_iota(I32, acc.shape, 1)
+        for i in range(8):
+            if first is not None:
+                acc = jnp.where(lanes == i, pltpu.roll(rows[i][part, :], (i - first) % Y, 1), acc)
+            if last is not None:
+                acc = jnp.where(lanes == 8 + i, pltpu.roll(rows[i][part, :], (8 + i - last) % Y, 1), acc)
+        return acc
+
+    from_start = reply([around(own, up_row[...], down_row[...], hvc_m[...], hvc_p[...], i) for i in range(8)])
     for i in range(8):
         base[i] = from_start[i]
 
@@ -477,32 +498,83 @@
         (copy(REPLY + 3, sc_m, hc_p, to_w), west, east),
     )
     edges = [launch(*c) for c in edges]
+
+    def code_of(v, eighths):
+        inverse = (32767.0 * 8.0) / eighths.astype(F32)
+        return ((v * inverse + 32768.5).astype(I32) - 32768).astype(I16)
+
+    def eighths_of(v):
+        return (jnp.max(jnp.abs(v), axis=0, keepdims=True) * 8.0).astype(I32) + 1
+
+    def send_piece(piece, rows, tile):
+        for n in range(SPAN):
+            gsend[piece, pl.ds(H * n, H), :] = rows[n]
+        gsend[piece, pl.ds(MARK, 16), :] = tile
+        out = []
+        for d in (2, 1, 3):
+            there = copy(GATHER + 3 * piece + d - 1, gsend.at[piece], grecv.at[piece, d - 1], at(zh, (y + d) % 4))
+            out.append((launch(there), piece, d))
+        return out
+
+    def closed(i, t):
+        return (cost[i] + t) * keep_rows[i:i + 1, :]
+
+    gathers = []
+    for piece in range(PIECES - 1):
+        indices = (2 * piece + 1, 2 * piece + 2)
+        twice = [closed(i, t) for i, t in zip(indices, reply([around(once, None, None, None, None, i) for i in indices]))]
+        eighths = eighths_of(jnp.concatenate(twice, axis=0))
+        tile = jnp.broadcast_to(eighths, (16, Y)).astype(I16)
+        gathers += send_piece(piece, [code_of(v, eighths) for v in twice], tile)
+    whole = slice(0, H)
+    sides = side_by_side(once, 0, Y - 1, whole)
+    cost_sides = side_by_side(cost, 0, Y - 1, whole)
+    inner_first = side_by_side(once, 1, None, slice(0, 32))
+    inner_last = side_by_side(once, None, Y - 2, slice(32, H))
+    after_sides, before_sides = pltpu.roll(sides, Y - 1, 1), pltpu.roll(sides, 1, 1)
     for n in edges:
         land(n)
-
+    last_three = reply((
+        around(once, hr_m[...], hr_p[...], hc_m[...], hc_p[...], 0),
+        around(once, hr_m[...], hr_p[...], hc_m[...], hc_p[...], 7),
+        (
+            sides, before_sides[16:48, :], (after_sides[0:16, :], after_sides[48:64, :]),
+            jnp.where(lane_of < 8, inner_first, pltpu.roll(hc_p[...], 8, 1)),
+            jnp.where(lane_of < 8, hc_m[...], inner_last), w_sides,
+        ),
+    ))
+    ends = (closed(0, last_three[0]), closed(7, last_three[1]))
+    columns = (cost_sides + last_three[2]) * keep_sides
+    patch = columns[0:8, :]
+    for n in range(1, 8):
+        here = jnp.logical_and(lane_8 >= 16 * n, lane_8 < 16 * n + 16)
+        patch = jnp.where(here, pltpu.roll(columns[8 * n:8 * n + 8, :], 16 * n, 1), patch)
+    eighths = eighths_of(jnp.concatenate(ends, axis=0))
+    eighths_patch = eighths_of(patch)
+    scales = jnp.where(row_8 < 4, eighths, eighths_patch)
+    inverse = (32767.0 * 8.0) / eighths_patch.astype(F32)
+    patch_code = (patch * inverse + 32768.5).astype(I32) - 32768
+    tile = jnp.concatenate([scales, patch_code], axis=0).astype(I16)
+    gathers += send_piece(PIECES - 1, [code_of(v, eighths) for v in ends], tile)
+
+    lane_w = lax.broadcasted_iota(I32, (H, Y), 1)
     out_rows = out.reshape(H * X, Y)
 
     def unpack(codes, qq, piece):
         scale = codes[MARK:MARK + 1, :].astype(F32) * (0.125 / 32767.0)
-        for n in range(SPAN):
-            v = codes[H * n:H * n + H, :].astype(F32) * scale
-            out_rows[pl.ds(qq * 8 + SPAN * piece + n, H, stride=X), :] = v
-
-    gathers = []
-    for piece in range(PIECES):
-        indices = range(SPAN * piece, SPAN * piece + SPAN)
-        twice = reply(once, hr_m[...], hr_p[...], hc_m[...], hc_p[...], indices)
-        twice = [(cost[i] + t) * keep_rows[i:i + 1, :] for i, t in zip(indices, twice)]
-        top = jnp.max(jnp.abs(jnp.concatenate(twice, axis=0)), axis=0, keepdims=True)
-        eighths = (top * 8.0).astype(I32) + 1
-        inverse = (32767.0 * 8.0) / eighths.astype(F32)
-        for n in range(SPAN):
-            code = (twice[n] * inverse + 32768.5).astype(I32) - 32768
-            gsend[piece, pl.ds(H * n, H), :] = code.astype(I16)
-        gsend[piece, pl.ds(MARK, 16), :] = jnp.broadcast_to(eighths, (16, Y)).astype(I16)
-        for d in (2, 1, 3):
-            there = copy(GATHER + 3 * piece + d - 1, gsend.at[piece], grecv.at[piece, d - 1], at(zh, (y + d) % 4))
-            gathers.append((launch(there), piece, d))
+        indices = (2 * piece + 1, 2 * piece + 2) if piece < PIECES - 1 else (0, 7)
+        for n, i in enumerate(indices):
+            out_rows[pl.ds(qq * 8 + i, H, stride=X), :] = codes[H * n:H * n + H, :].astype(F32) * scale
+        if piece < PIECES - 1:
+            return
+        scale = codes[MARK + 4:MARK + 5, :].astype(F32) * (0.125 / 32767.0)
+        flat = codes[MARK + 8:MARK + 16, :].astype(F32) * scale
+        wide = jnp.concatenate([pltpu.roll(flat, Y - 16 * n, 1) if n else flat for n in range(8)], axis=0)
+        for i in range(1, 7):
+            at_row = pl.ds(qq * 8 + i, H, stride=X)
+            v = jnp.where(lane_w == 0, pltpu.roll(wide, Y - i, 1), out_rows[at_row, :])
+            out_rows[at_row, :] = jnp.where(lane_w == Y - 1, pltpu.roll(wide, Y - 9 - i, 1), v)
+
     for piece in range(PIECES):
         unpack(gsend[piece].astype(I32), q, piece)
     for n, piece, d in gathers:
@@ -530,8 +602,8 @@
     scratch = [
         vmem(H, X, Y), pltpu.VMEM((H, X, Y), BF16), vmem(H, X, Y), pltpu.VMEM((X, Y), I32), vmem(H, Y), vmem(H, Y),
         vmem(H, H), vmem(H, H),
-        vmem(40, Y), vmem(40, Y), vmem(64, Y), vmem(64, Y), vmem(32, Y), vmem(32, Y),
-        vmem(40, Y), vmem(40, Y), vmem(64, Y), vmem(64, Y), vmem(32, Y), vmem(32, Y),
+        vmem(40, Y), vmem(40, Y), *[vmem(32, Y) for _ in range(6)],
+        vmem(40, Y), vmem(40, Y), *[vmem(32, Y) for _ in range(6)],
         vmem(H, X, Y), vmem(4, 16, Y), vmem(4, X, Y), vmem(4, 16, Y), vmem(4, X, Y), vmem(4, X, Y),
         vmem(X, Y),
         pltpu.VMEM((CHUNKS, 3, ROWS, Y), I16), pltpu.VMEM((CHUNKS, 3, ROWS, Y), I16),

time: 54.4 us -> 51.6 us (0.949)
  the two profiles are of different devices: /device:TPU:10 before, /device:TPU:2 now
where the time goes in v3:
time: 51.6 us; the launch traced here: 51.5 us
  Pallas kernels  50.8 us (98%)
  between operations  0.64 us (1%)
    pallas_call x1, Pallas kernels, shards(): pl.pallas_call(kernel, out_shape=(held, held), in_specs=[in_hbm] * 9, out...  49.5 us
    pallas_call x1, Pallas kernels, shards(): pl.pallas_call(write_out, out_shape=(whole, whole), in_specs=[in_vmem, in...  1.33 us

profile of v3, /device:TPU:2, one launch (start us, length us, event | category | flops | bytes accessed | tf_op | source)
XLA Modules:
  0.0 51.5 jit_solution(10616009420416751189)
XLA Ops:
  0.6 49.5 %play.1 = (f32[64,32,128]{2,1,0:T(8,128)S(1)}, f32[64,32,128]{2,1,0:T(8,128)S(1)}) custom-call(s32[16]{0:T(128)} %counts_hbm.1, f32[64,32,128]{2,1,0:T(8,128)} %bitcast.3, bf16[64,32,128]{2,1,0:T(8,128)(2,1)} %bitcast.4, f32[64,32,128]{2,1,0:T(8,128)} %value_hbm.1, s32[32,128]{1,0:T(8,128)} %labels_hbm.1, f32[64,128]{1,0:T(8,128)} %constant.6.clone.ax_hbm, ...), custom_call_target="tpu_custom_call" | custom-call | tf_op jit(solution)/shard_map/play/pallas_call | solution.py:623
  50.1 1.3 %write.1 = (f32[64,32,128]{2,1,0:T(8,128)}, f32[64,32,128]{2,1,0:T(8,128)}) custom-call(f32[64,32,128]{2,1,0:T(8,128)S(1)} %get-tuple-element.6.moved, f32[64,32,128]{2,1,0:T(8,128)S(1)} %get-tuple-element.7.values), custom_call_target="tpu_custom_call" | custom-call | tf_op jit(solution)/shard_map/write/pallas_call | solution.py:635

commit v4 on v3

--- a/solution.py
+++ b/solution.py
@@ -71,7 +71,7 @@
     up_row, down_row, cs, kf, cf,
     sr_m, sr_p, sc_m, sc_p, hr_m, hr_p, hc_m, hc_p,
     gsend, grecv,
-    counts, load_sem, ss, rs,
+    counts, word, load_sem, ss, rs,
 ):
     member = lax.axis_index("member")
     gx = lax.axis_index("gx")
@@ -86,8 +86,23 @@
 
     pair = (jnp.where(zh % 2 == 0, zh + 1, zh - 1), 3 - zh)
 
+    quads = [pl.ds(16 * k, 16) for k in (0, 3, 1, 2)]
+    loads = [
+        pltpu.make_async_copy(src, dst, load_sem.at[i])
+        for i, (src, dst) in enumerate((
+            *[(density.at[b], r0.at[b]) for b in quads],
+            (labels_hbm, labels), (turn_hbm, turn), (value_hbm, val), (ax_hbm, axt), (ay_hbm, ayt),
+            (coupling_hbm, coupling), (kernel_hbm, kern), (counts_hbm, counts),
+        ))
+    ]
+    for c in loads[:5]:
+        c.start()
+
     barrier = pltpu.get_barrier_semaphore()
-    greeted = [at(zh, (y + d) % 4) for d in (1, 2, 3)] + [at(p, y) for p in pair]
+    z_lo, core = gx // 2, gx % 2
+    z_up, z_down = (zh * 4 + z_lo + 1) % 16, (zh * 4 + z_lo + 15) % 16
+    beside = [{"member": (z // 4) * 4 + y, "gx": (z % 4) * 2 + core} for z in (z_up, z_down)]
+    greeted = [at(zh, (y + d) % 4) for d in (1, 2, 3)] + beside
     greeted += [{"gy": (gy + d) % 4} for d in (1, 3)]
 
     def greet(target):
@@ -102,15 +117,7 @@
     for target in greeted:
         greet(target)
 
-    loads = [
-        pltpu.make_async_copy(src, dst, load_sem.at[i])
-        for i, (src, dst) in enumerate((
-            (density, r0), (labels_hbm, labels), (value_hbm, val), (turn_hbm, turn), (ax_hbm, axt), (ay_hbm, ayt),
-            (coupling_hbm, coupling), (kernel_hbm, kern),
-            (counts_hbm, counts),
-        ))
-    ]
-    for c in loads:
+    for c in loads[5:]:
         c.start()
 
     def copy(i, src, dst, target):
@@ -138,8 +145,8 @@
         shift = position + 1 if k in (0, 1) else position
         return jnp.where(lane == position, pltpu.roll(r, shift, 1), acc)
 
-    loads[0].wait()
-    loads[1].wait()
+    for c in loads[:5]:
+        c.wait()
     opened = jnp.where(labels[...] != 1, 1.0, 0.0).astype(F32)
     keep[...] = jnp.where(labels[...] == 2, 0.0, 1.0).astype(F32)
     zero_plane = jnp.zeros((X, Y), F32)
@@ -204,13 +211,28 @@
         guarded(receives, c.wait_recv)
         landed.add(n)
 
+    sent = set()
+
+    def settle(upto):
+        for n in range(upto):
+            if n not in sent:
+                c, sends, _ = started[n]
+                guarded(sends, c.wait_send)
+                sent.add(n)
+
     def finish_all():
-        for n, (c, sends, _) in enumerate(started):
+        for n in range(len(started)):
             if n not in landed:
                 land(n)
-            guarded(sends, c.wait_send)
+        settle(len(started))
 
     pl.semaphore_wait(barrier, len(greeted) + has_m.astype(I32) + has_p.astype(I32))
+
+    def pass_word(n):
+        for target in beside:
+            pl.semaphore_signal(word.at[n], inc=1, device_id=target, device_id_type=MESH)
+
+    pass_word(0)
     begun = [launch(*c) for c in first[:4]]
     @pl.when(gx == 0)
     def _():
@@ -244,7 +266,7 @@
     def _():
         hr_p[...] = jnp.zeros((32, Y), F32)
 
-    loads[2].wait()
+    loads[6].wait()
     own = [value_row(i) for i in range(8)]
     svc_p[...] = pack_values(own, 32, True)
     svc_m[...] = pack_values(own, 0, False)
@@ -252,8 +274,8 @@
     sv_m[0:16, :] = own[0][0:16, :]
     sv_m[16:32, :] = own[0][48:64, :]
     begun += [launch(*c) for c in first[4:]]
-    for c in loads[3:]:
-        c.wait()
+    for n in (5, 7, 8, 9, 10, 11):
+        loads[n].wait()
     kf[:, 0:64] = kern[...]
     kf[:, 64:128] = kern[...]
     for n in begun[:4]:
@@ -326,6 +348,9 @@
         second.append(launch(copy(STEP_ROW + k, s2x.at[k], h2x.at[k], target[0]), *target[1:]))
         target = (to_e, east, west) if k in (0, 1) else (to_w, west, east)
         second.append(launch(copy(STEP_COL + k, s2y.at[k], h2y.at[k], target[0]), *target[1:]))
+
+    pl.semaphore_wait(word.at[0], 2)
+    pass_word(1)
 
     over_y = [[] for _ in range(CHUNKS)]
     for k in range(4):
@@ -340,6 +365,8 @@
                 ysend[c, d - 1] = encode(part.reshape(ROWS, Y) * (1.0 / BOUND))
                 there = copy(OVER_Y + 3 * c + d - 1, ysend.at[c, d - 1], yrecv.at[c, d - 1], at(zh, yy))
                 over_y[c].append(launch(there))
+    pl.semaphore_wait(word.at[1], 2)
+    pass_word(2)
 
     def count(z, yy):
         return counts[z * 4 + yy].astype(F32)
@@ -358,6 +385,7 @@
     def scaled(part, factor):
         return (part.reshape(CHUNK, 8, Y) * factor).reshape(ROWS, Y)
 
+    pl.semaphore_wait(word.at[2], 2)
     over_z = [[None, None] for _ in range(CHUNKS)]
     for c in range(CHUNKS):
         block = pl.ds(CHUNK * c, CHUNK)
@@ -497,6 +525,7 @@
         (copy(REPLY + 2, sc_p, hc_m, to_e), east, west),
         (copy(REPLY + 3, sc_m, hc_p, to_w), west, east),
     )
+    before_edges = len(started)
     edges = [launch(*c) for c in edges]
 
     def code_of(v, eighths):
@@ -526,6 +555,7 @@
         eighths = eighths_of(jnp.concatenate(twice, axis=0))
         tile = jnp.broadcast_to(eighths, (16, Y)).astype(I16)
         gathers += send_piece(piece, [code_of(v, eighths) for v in twice], tile)
+    settle(before_edges)
     whole = slice(0, H)
     sides = side_by_side(once, 0, Y - 1, whole)
     cost_sides = side_by_side(cost, 0, Y - 1, whole)
@@ -577,6 +607,7 @@
 
     for piece in range(PIECES):
         unpack(gsend[piece].astype(I32), q, piece)
+    settle(len(started) - 3)
     for n, piece, d in gathers:
         land(n)
         yy = (y + 4 - d) % 4
@@ -611,7 +642,7 @@
         vmem(32, Y), vmem(32, Y), vmem(8, Y), vmem(H, 128), vmem(H, 128),
         *[vmem(32, Y) for _ in range(8)],
         pltpu.VMEM((PIECES, MARK + 16, Y), I16), pltpu.VMEM((PIECES, 3, MARK + 16, Y), I16),
-        pltpu.SMEM((16,), I32), pltpu.SemaphoreType.DMA((9,)),
+        pltpu.SMEM((16,), I32), pltpu.SemaphoreType.REGULAR((3,)), pltpu.SemaphoreType.DMA((12,)),
         pltpu.SemaphoreType.DMA((COPIES,)), pltpu.SemaphoreType.DMA((COPIES,)),
     ]
     held = pltpu.VMEM((H, X, Y), F32)

time: 51.6 us -> 50.9 us (0.986)
  the two profiles are of different devices: /device:TPU:2 before, /device:TPU:4 now
where the time goes in v4:
time: 50.9 us; the launch traced here: 50.7 us
  Pallas kernels  50.1 us (98%)
  between operations  0.64 us (1%)
    pallas_call x1, Pallas kernels, shards(): pl.pallas_call(kernel, out_shape=(held, held), in_specs=[in_hbm] * 9, out...  48.7 us
    pallas_call x1, Pallas kernels, shards(): pl.pallas_call(write_out, out_shape=(whole, whole), in_specs=[in_vmem, in...  1.33 us

profile of v4, /device:TPU:4, one launch (start us, length us, event | category | flops | bytes accessed | tf_op | source)
XLA Modules:
  0.0 50.7 jit_solution(3449109490467257544)
XLA Ops:
  0.6 48.7 %play.1 = (f32[64,32,128]{2,1,0:T(8,128)S(1)}, f32[64,32,128]{2,1,0:T(8,128)S(1)}) custom-call(s32[16]{0:T(128)} %counts_hbm.1, f32[64,32,128]{2,1,0:T(8,128)} %bitcast.3, bf16[64,32,128]{2,1,0:T(8,128)(2,1)} %bitcast.4, f32[64,32,128]{2,1,0:T(8,128)} %value_hbm.1, s32[32,128]{1,0:T(8,128)} %labels_hbm.1, f32[64,128]{1,0:T(8,128)} %constant.6.clone.ax_hbm, ...), custom_call_target="tpu_custom_call" | custom-call | tf_op jit(solution)/shard_map/play/pallas_call | solution.py:654
  49.4 1.3 %write.1 = (f32[64,32,128]{2,1,0:T(8,128)}, f32[64,32,128]{2,1,0:T(8,128)}) custom-call(f32[64,32,128]{2,1,0:T(8,128)S(1)} %get-tuple-element.6.moved, f32[64,32,128]{2,1,0:T(8,128)S(1)} %get-tuple-element.7.values), custom_call_target="tpu_custom_call" | custom-call | tf_op jit(solution)/shard_map/write/pallas_call | solution.py:666

commit v5 on v4

--- a/solution.py
+++ b/solution.py
@@ -71,7 +71,7 @@
     up_row, down_row, cs, kf, cf,
     sr_m, sr_p, sc_m, sc_p, hr_m, hr_p, hc_m, hc_p,
     gsend, grecv,
-    counts, word, load_sem, ss, rs,
+    counts, word, word_y, load_sem, ss, rs,
 ):
     member = lax.axis_index("member")
     gx = lax.axis_index("gx")
@@ -102,7 +102,8 @@
     z_lo, core = gx // 2, gx % 2
     z_up, z_down = (zh * 4 + z_lo + 1) % 16, (zh * 4 + z_lo + 15) % 16
     beside = [{"member": (z // 4) * 4 + y, "gx": (z % 4) * 2 + core} for z in (z_up, z_down)]
-    greeted = [at(zh, (y + d) % 4) for d in (1, 2, 3)] + beside
+    beside_y = [at(zh, (y + d) % 4) for d in (1, 3)]
+    greeted = beside_y + beside
     greeted += [{"gy": (gy + d) % 4} for d in (1, 3)]
 
     def greet(target):
@@ -233,6 +234,8 @@
             pl.semaphore_signal(word.at[n], inc=1, device_id=target, device_id_type=MESH)
 
     pass_word(0)
+    for target in beside_y:
+        pl.semaphore_signal(word_y, inc=1, device_id=target, device_id_type=MESH)
     begun = [launch(*c) for c in first[:4]]
     @pl.when(gx == 0)
     def _():
@@ -349,6 +352,7 @@
         target = (to_e, east, west) if k in (0, 1) else (to_w, west, east)
         second.append(launch(copy(STEP_COL + k, s2y.at[k], h2y.at[k], target[0]), *target[1:]))
 
+    pl.semaphore_wait(word_y, 2)
     pl.semaphore_wait(word.at[0], 2)
     pass_word(1)
 
@@ -517,16 +521,15 @@
     sr_p[...] = once[7][16:48, :]
     sr_m[0:16, :] = once[0][0:16, :]
     sr_m[16:32, :] = once[0][48:64, :]
+    before_edges = len(started)
+    edges = [
+        launch(copy(REPLY, sr_p, hr_m, near_down), has_down, has_up),
+        launch(copy(REPLY + 1, sr_m, hr_p, near_up), has_up, has_down),
+    ]
     sc_p[...] = pack_values(once, 32, True)
+    edges.append(launch(copy(REPLY + 2, sc_p, hc_m, to_e), east, west))
     sc_m[...] = pack_values(once, 0, False)
-    edges = (
-        (copy(REPLY, sr_p, hr_m, near_down), has_down, has_up),
-        (copy(REPLY + 1, sr_m, hr_p, near_up), has_up, has_down),
-        (copy(REPLY + 2, sc_p, hc_m, to_e), east, west),
-        (copy(REPLY + 3, sc_m, hc_p, to_w), west, east),
-    )
-    before_edges = len(started)
-    edges = [launch(*c) for c in edges]
+    edges.append(launch(copy(REPLY + 3, sc_m, hc_p, to_w), west, east))
 
     def code_of(v, eighths):
         inverse = (32767.0 * 8.0) / eighths.astype(F32)
@@ -608,7 +611,7 @@
     for piece in range(PIECES):
         unpack(gsend[piece].astype(I32), q, piece)
     settle(len(started) - 3)
-    for n, piece, d in gathers:
+    for n, piece, d in sorted(gathers, key=lambda g: (g[1], g[2] == 2)):
         land(n)
         yy = (y + 4 - d) % 4
         unpack(grecv[piece, d - 1].astype(I32), jnp.where(odd == 1, 3 - yy, yy), piece)
@@ -642,7 +645,7 @@
         vmem(32, Y), vmem(32, Y), vmem(8, Y), vmem(H, 128), vmem(H, 128),
         *[vmem(32, Y) for _ in range(8)],
         pltpu.VMEM((PIECES, MARK + 16, Y), I16), pltpu.VMEM((PIECES, 3, MARK + 16, Y), I16),
-        pltpu.SMEM((16,), I32), pltpu.SemaphoreType.REGULAR((3,)), pltpu.SemaphoreType.DMA((12,)),
+        pltpu.SMEM((16,), I32), pltpu.SemaphoreType.REGULAR((3,)), pltpu.SemaphoreType.REGULAR, pltpu.SemaphoreType.DMA((12,)),
         pltpu.SemaphoreType.DMA((COPIES,)), pltpu.SemaphoreType.DMA((COPIES,)),
     ]
     held = pltpu.VMEM((H, X, Y), F32)

time: 50.9 us -> 50.3 us (0.988)
  the two profiles are of different devices: /device:TPU:4 before, /device:TPU:34 now
where the time goes in v5:
time: 50.3 us; the launch traced here: 50.2 us
  Pallas kernels  49.5 us (98%)
  between operations  0.64 us (1%)
    pallas_call x1, Pallas kernels, shards(): pl.pallas_call(kernel, out_shape=(held, held), in_specs=[in_hbm] * 9, out...  48.2 us
    pallas_call x1, Pallas kernels, shards(): pl.pallas_call(write_out, out_shape=(whole, whole), in_specs=[in_vmem, in...  1.33 us

profile of v5, /device:TPU:34, one launch (start us, length us, event | category | flops | bytes accessed | tf_op | source)
XLA Modules:
  0.0 50.2 jit_solution(16075732421299264416)
XLA Ops:
  0.6 48.2 %play.1 = (f32[64,32,128]{2,1,0:T(8,128)S(1)}, f32[64,32,128]{2,1,0:T(8,128)S(1)}) custom-call(s32[16]{0:T(128)} %counts_hbm.1, f32[64,32,128]{2,1,0:T(8,128)} %bitcast.3, bf16[64,32,128]{2,1,0:T(8,128)(2,1)} %bitcast.4, f32[64,32,128]{2,1,0:T(8,128)} %value_hbm.1, s32[32,128]{1,0:T(8,128)} %labels_hbm.1, f32[64,128]{1,0:T(8,128)} %constant.6.clone.ax_hbm, ...), custom_call_target="tpu_custom_call" | custom-call | tf_op jit(solution)/shard_map/play/pallas_call | solution.py:657
  48.8 1.3 %write.1 = (f32[64,32,128]{2,1,0:T(8,128)}, f32[64,32,128]{2,1,0:T(8,128)}) custom-call(f32[64,32,128]{2,1,0:T(8,128)S(1)} %get-tuple-element.6.moved, f32[64,32,128]{2,1,0:T(8,128)S(1)} %get-tuple-element.7.values), custom_call_target="tpu_custom_call" | custom-call | tf_op jit(solution)/shard_map/write/pallas_call | solution.py:669

commit v6 on v5

--- a/solution.py
+++ b/solution.py
@@ -389,17 +389,6 @@
     def scaled(part, factor):
         return (part.reshape(CHUNK, 8, Y) * factor).reshape(ROWS, Y)
 
-    pl.semaphore_wait(word.at[2], 2)
-    over_z = [[None, None] for _ in range(CHUNKS)]
-    for c in range(CHUNKS):
-        block = pl.ds(CHUNK * c, CHUNK)
-        part = r2[block, pl.ds(pl.multiple_of(q * 8, 8), 8), :].reshape(ROWS, Y) * count(zh, y)
-        for n, d in zip(over_y[c], (2, 1, 3)):
-            land(n)
-            part = part + decode(yrecv[c, d - 1]) * count(zh, (y + 4 - d) % 4)
-        zsend[c, 0] = encode(scaled(part, inverse_mine))
-        over_z[c][0] = launch(copy(OVER_Z + 2 * c, zsend.at[c, 0], zrecv.at[c, 0], at(pair[c % 2], y)))
-
     for n in begun[4:]:
         land(n)
 
@@ -490,6 +479,17 @@
     from_start = reply([around(own, up_row[...], down_row[...], hvc_m[...], hvc_p[...], i) for i in range(8)])
     for i in range(8):
         base[i] = from_start[i]
+
+    pl.semaphore_wait(word.at[2], 2)
+    over_z = [[None, None] for _ in range(CHUNKS)]
+    for c in range(CHUNKS):
+        block = pl.ds(CHUNK * c, CHUNK)
+        part = r2[block, pl.ds(pl.multiple_of(q * 8, 8), 8), :].reshape(ROWS, Y) * count(zh, y)
+        for n, d in zip(over_y[c], (2, 1, 3)):
+            land(n)
+            part = part + decode(yrecv[c, d - 1]) * count(zh, (y + 4 - d) % 4)
+        zsend[c, 0] = encode(scaled(part, inverse_mine))
+        over_z[c][0] = launch(copy(OVER_Z + 2 * c, zsend.at[c, 0], zrecv.at[c, 0], at(pair[c % 2], y)))
 
     lower = [jnp.full((8, Y), zh, I32) < jnp.full((8, Y), p, I32) for p in pair]
 

time: 50.3 us -> 50.5 us (level)
  the two profiles are of different devices: /device:TPU:34 before, /device:TPU:36 now
where the time goes in v6:
time: 50.5 us; the launch traced here: 50.4 us
  Pallas kernels  49.8 us (99%)
  between operations  0.64 us (1%)
    pallas_call x1, Pallas kernels, shards(): pl.pallas_call(kernel, out_shape=(held, held), in_specs=[in_hbm] * 9, out...  48.4 us
    pallas_call x1, Pallas kernels, shards(): pl.pallas_call(write_out, out_shape=(whole, whole), in_specs=[in_vmem, in...  1.33 us

profile of v6, /device:TPU:36, one launch (start us, length us, event | category | flops | bytes accessed | tf_op | source)
XLA Modules:
  0.0 50.4 jit_solution(5636967245336229922)
XLA Ops:
  0.6 48.4 %play.1 = (f32[64,32,128]{2,1,0:T(8,128)S(1)}, f32[64,32,128]{2,1,0:T(8,128)S(1)}) custom-call(s32[16]{0:T(128)} %counts_hbm.1, f32[64,32,128]{2,1,0:T(8,128)} %bitcast.3, bf16[64,32,128]{2,1,0:T(8,128)(2,1)} %bitcast.4, f32[64,32,128]{2,1,0:T(8,128)} %value_hbm.1, s32[32,128]{1,0:T(8,128)} %labels_hbm.1, f32[64,128]{1,0:T(8,128)} %constant.6.clone.ax_hbm, ...), custom_call_target="tpu_custom_call" | custom-call | tf_op jit(solution)/shard_map/play/pallas_call | solution.py:657
  49.1 1.3 %write.1 = (f32[64,32,128]{2,1,0:T(8,128)}, f32[64,32,128]{2,1,0:T(8,128)}) custom-call(f32[64,32,128]{2,1,0:T(8,128)S(1)} %get-tuple-element.6.moved, f32[64,32,128]{2,1,0:T(8,128)S(1)} %get-tuple-element.7.values), custom_call_target="tpu_custom_call" | custom-call | tf_op jit(solution)/shard_map/write/pallas_call | solution.py:669
